TPU v7x, 512 devices: a whole 4x8x8 slice. The times are simulated.
512 devices in a mesh: pool: 32 (over x, y), head: 16 (over z, core).
Axes of the slice: x: 4, y: 8, z: 8, core: 2. Of those that a mesh axis runs over, the one named last changes fastest.
Arguments:
- queries: bfloat16 [1024, 8192], P('pool', 'head'), may hold values from -120 to 120, as said below
- branch_prefix: int32 [1024], replicated, may hold values from 0 to 15
- stretch_table: int32 [256], P('pool'), may hold values from 0 to 255, each once
- suffix_len: int32 [1024], P('pool'), may hold values from 1 to 128, 65536 in all
- prefix_keys: bfloat16 [16, 32768, 128], P('head', 'pool'), may hold values from -4 to 4, as said below
- prefix_values: bfloat16 [16, 32768, 128], P('head', 'pool'), may hold values from -4 to 4, as said below
- suffix_keys: bfloat16 [16, 1024, 128, 128], P('head', 'pool'), may hold values from -4 to 4, as said below
- suffix_values: bfloat16 [16, 1024, 128, 128], P('head', 'pool'), may hold values from -4 to 4, as said below
- out_weight: bfloat16 [8192, 8192], P('head', 'pool'), may hold values from -0.14941406 to 0.14941406
Outputs:
- mixed: bfloat16 [1024, 8192], P('head', 'pool')
Inputs may be any that keep to these rules, and one draw needn't show every extreme that they name: `queries`: row b holds branch b's 64 query heads in order, 128 entries each. `branch_prefix`: the prefix that each branch extends. Slot s holds block stretch_table[s] % 16 of prefix stretch_table[s] // 16; each value appears once. `suffix_len`: counts the branch's own new key; some branch has 128. `prefix_keys`: stored head h is key-value head h * 8 // 16 of the model; copies of one head are equal. `prefix_values`: stored head h is key-value head h * 8 // 16 of the model; copies of one head are equal. `suffix_keys`: stored head h is key-value head h * 8 // 16 of the model; copies of one head are equal. `suffix_values`: stored head h is key-value head h * 8 // 16 of the model; copies of one head are equal.
All inputs are finite; a program needn't handle non-finite values. No bound on the sum of `suffix_len` on one device may be relied on, other than what follows from the above.
Results may differ from a plain program's by a relative error of at most 0.0051.
Values may be sent and summed in bfloat16 or wider, within the bound.
No kernel may reach another device: no remote copies, remote signals or barrier semaphores. Data moves between devices by JAX's collectives and lax.ppermute only.
A program may use at most 64 MiB of HBM per device.

v0:
```python
import math

import jax
import jax.numpy as jnp
from jax import lax
from jax.sharding import PartitionSpec as P

CPP = 16


masked_score = -1e30


def soft_partial(scores, visible, values, form):
    scores = jnp.where(visible, scores, masked_score)
    highest = jnp.max(scores, axis=-1)
    weights = jnp.where(visible, jnp.exp(scores - highest[..., None]), 0.0)
    totals = jnp.sum(weights, axis=-1)
    numerator = jnp.einsum(
        form, weights.astype(jnp.bfloat16), values, preferred_element_type=jnp.float32
    )
    return (highest, totals, numerator)


def on_device(
    queries,
    branch_prefix,
    stretch_table,
    suffix_len,
    prefix_keys,
    prefix_values,
    suffix_keys,
    suffix_values,
    out_weight,
):
    head_size = prefix_keys.shape[2]
    kv_local = prefix_keys.shape[0]
    local_heads = queries.shape[1] // head_size
    group_size = local_heads // kv_local
    home_rows = queries.shape[0]
    score_scale = 1.0 / math.sqrt(head_size)
    suffix_span = suffix_keys.shape[2]
    query_home = queries.reshape(home_rows, kv_local, group_size, head_size)
    visible_suffix = (jnp.arange(suffix_span, dtype=jnp.int32)[None, :] < suffix_len[:, None])[
        :, None, None, :
    ]
    suffix_scores = (
        jnp.einsum("bkgd,kbtd->bkgt", query_home, suffix_keys, preferred_element_type=jnp.float32)
        * score_scale
    )
    suffix_high, suffix_totals, suffix_numer = soft_partial(
        suffix_scores, visible_suffix, suffix_values, "bkgt,kbtd->bkgd"
    )
    suffix_high = suffix_high.reshape(home_rows, local_heads)
    suffix_totals = suffix_totals.reshape(home_rows, local_heads)
    suffix_numer = suffix_numer.reshape(home_rows, local_heads, head_size)
    gathered = lax.all_gather(queries, "pool", axis=0, tiled=True)
    branches = gathered.shape[0]
    slot_count = stretch_table.shape[0]
    stretch_len = prefix_keys.shape[1] // slot_count
    token_prefix = jnp.repeat(stretch_table // CPP, stretch_len)
    block_rows = math.gcd(branches, 512)

    def owner_block(operands):
        query_block, prefix_block = operands
        query_block = query_block.reshape(block_rows, kv_local, group_size, head_size)
        scores = (
            jnp.einsum(
                "bkgd,ktd->bkgt", query_block, prefix_keys, preferred_element_type=jnp.float32
            )
            * score_scale
        )
        visible = (prefix_block[:, None] == token_prefix[None, :])[:, None, None, :]
        return soft_partial(scores, visible, prefix_values, "bkgt,ktd->bkgd")

    owner_high, owner_totals, owner_numer = lax.map(
        owner_block,
        (
            gathered.reshape(branches // block_rows, block_rows, local_heads * head_size),
            branch_prefix.reshape(branches // block_rows, block_rows),
        ),
    )
    owner_high = owner_high.reshape(branches, local_heads)
    owner_totals = owner_totals.reshape(branches, local_heads)
    owner_numer = owner_numer.reshape(branches, local_heads, head_size)
    pool_size = lax.axis_size("pool")
    got_high, got_totals, got_numer = (
        lax.all_to_all(
            owner_high.reshape(pool_size, home_rows, local_heads),
            "pool",
            split_axis=0,
            concat_axis=0,
            tiled=True,
        ),
        lax.all_to_all(
            owner_totals.reshape(pool_size, home_rows, local_heads),
            "pool",
            split_axis=0,
            concat_axis=0,
            tiled=True,
        ),
        lax.all_to_all(
            owner_numer.reshape(pool_size, home_rows, local_heads, head_size),
            "pool",
            split_axis=0,
            concat_axis=0,
            tiled=True,
        ),
    )
    overall = jnp.maximum(suffix_high, jnp.max(got_high, axis=0))
    factors = jnp.exp(got_high - overall[None])
    own_factor = jnp.exp(suffix_high - overall)
    denominator = suffix_totals * own_factor + jnp.sum(got_totals * factors, axis=0)
    numerator = suffix_numer * own_factor[..., None] + jnp.sum(
        got_numer * factors[..., None], axis=0
    )
    attention = (
        (numerator / denominator[..., None])
        .reshape(home_rows, local_heads * head_size)
        .astype(jnp.bfloat16)
    )
    everything = lax.all_gather(attention, "pool", axis=0, tiled=True)
    return lax.psum_scatter(
        jnp.dot(everything, out_weight, preferred_element_type=jnp.float32),
        "head",
        scatter_dimension=0,
        tiled=True,
    ).astype(jnp.bfloat16)


def solution(mesh):
    in_specs = (
        P("pool", "head"),
        P(),
        P("pool"),
        P("pool"),
        P("head", "pool", None),
        P("head", "pool", None),
        P("head", "pool", None, None),
        P("head", "pool", None, None),
        P("head", "pool"),
    )
    out_specs = P("head", "pool")
    return jax.shard_map(
        on_device, mesh=mesh, in_specs=in_specs, out_specs=out_specs, check_vma=False
    )
```

profile of v0, /device:TPU:2, one launch (start us, length us, event | category | flops | bytes accessed | tf_op | source)
XLA Modules:
  0.0 366.3 jit_solution(16578190147768019190)
XLA Ops:
  6.5 0.7 all-gather.3.cloned.1.call-update
  7.3 0.7 reshape.154
  8.6 86.8 %all-gather.3.cloned.1.call-done = bf16[1024,512]{1,0:T(8,128)(2,1)} async-done(((bf16[32,512]{1,0:T(8,128)(2,1)}), bf16[1024,512]{1,0:T(8,128)(2,1)}) %all-gather.3.cloned.1.call-update) | async-done | bytes 1048592 | tf_op jit(solution)/shard_map/all_gather | solution.py:57
  95.5 39.9 %while.15 = (s32[]{:T(128)}, f32[2,512,1,4]{1,0,3,2:T(2,128)S(1)}, f32[2,512,1,4]{1,0,3,2:T(2,128)S(1)}, f32[2,512,1,4,128]{4,1,0,3,2:T(8,128)}, s32[2,512]{1,0:...) while((s32[]{:T(128)}, f32[2,512,1,4]{1,0,3,2:T(2,128)S(1)}, ...), condition=%wide.region_4.5_spmd.clone, body=%wide.region_1.4_spmd.clone.sunk | while | flops 1101524992 | bytes 32618692 | solution.py:76
  95.9 1.1 constant_dynamic-slice_fusion.5
  97.2 6.0 %fusion.49 = (f32[512,4]{0,1:T(4,128)S(1)}, f32[512,4,1024]{2,0,1:T(8,128)}) fusion(pred[512,1024]{1,0:T(8,128)(4,1)S(1)} %broadcast_compare_fusion.2, bf16[512,4,128]{0,2,1:T(8,128)(2,1)S(1)} %bitcast.115, bf16[1,1024,128]{2,1,0:T(8,128)(2,1)} %get-tuple-element.227), kind=kOutput, calls=%fused_computation.3.clone.1 | convolution fusion | flops 543160320 | bytes 9707520 | tf_op jit(solution)/shard_map/while/body/eval_jaxpr/bkgd,ktd->bkgt/dot_general | solution.py:68
  103.3 5.1 %fusion.50 = f32[512,4]{0,1:T(4,128)S(1)} fusion(f32[512,4,1024]{2,0,1:T(8,128)} %get-tuple-element.198, f32[512,4]{0,1:T(4,128)S(1)} %get-tuple-element.197, pred[512,1024]{1,0:T(8,128)(4,1)S(1)} %broadcast_compare_fusion.2), kind=kLoop, calls=%fused_computation.5.clone.1 | loop fusion | flops 10483712 | bytes 8929280 | tf_op jit(solution)/shard_map/while/body/eval_jaxpr/reduce_sum | solution.py:18
  108.5 6.9 %fusion.51 = f32[2,512,1,4,128]{4,1,0,3,2:T(8,128)} fusion(f32[2,512,1,4,128]{4,1,0,3,2:T(8,128)} %get-tuple-element.213, s32[]{:T(128)S(6)} %copy.103, f32[512,4,1024]{2,0,1:T(8,128)} %get-tuple-element.198, f32[512,4]{0,1:T(4,128)S(1)} %get-tuple-element.197, pred[512,1024]{1,0:T(8,128)(4,1)S(1)} %broadcast_compare_fusion.2, ...), kind=kOutput, calls=%fused_computation.10.clone.1 | convolution fusion | flops 547356672 | bytes 10231812 | tf_op jit(solution)/shard_map/while/body/eval_jaxpr/bkgt,ktd->bkgd/dot_general | solution.py:19
  115.9 1.1 constant_dynamic-slice_fusion.5
  117.2 6.0 %fusion.49 = (f32[512,4]{0,1:T(4,128)S(1)}, f32[512,4,1024]{2,0,1:T(8,128)}) fusion(pred[512,1024]{1,0:T(8,128)(4,1)S(1)} %broadcast_compare_fusion.2, bf16[512,4,128]{0,2,1:T(8,128)(2,1)S(1)} %bitcast.115, bf16[1,1024,128]{2,1,0:T(8,128)(2,1)} %get-tuple-element.227), kind=kOutput, calls=%fused_computation.3.clone.1 | convolution fusion | flops 543160320 | bytes 9707520 | tf_op jit(solution)/shard_map/while/body/eval_jaxpr/bkgd,ktd->bkgt/dot_general | solution.py:68
  123.2 5.1 %fusion.50 = f32[512,4]{0,1:T(4,128)S(1)} fusion(f32[512,4,1024]{2,0,1:T(8,128)} %get-tuple-element.198, f32[512,4]{0,1:T(4,128)S(1)} %get-tuple-element.197, pred[512,1024]{1,0:T(8,128)(4,1)S(1)} %broadcast_compare_fusion.2), kind=kLoop, calls=%fused_computation.5.clone.1 | loop fusion | flops 10483712 | bytes 8929280 | tf_op jit(solution)/shard_map/while/body/eval_jaxpr/reduce_sum | solution.py:18
  128.5 6.9 %fusion.51 = f32[2,512,1,4,128]{4,1,0,3,2:T(8,128)} fusion(f32[2,512,1,4,128]{4,1,0,3,2:T(8,128)} %get-tuple-element.213, s32[]{:T(128)S(6)} %copy.103, f32[512,4,1024]{2,0,1:T(8,128)} %get-tuple-element.198, f32[512,4]{0,1:T(4,128)S(1)} %get-tuple-element.197, pred[512,1024]{1,0:T(8,128)(4,1)S(1)} %broadcast_compare_fusion.2, ...), kind=kOutput, calls=%fused_computation.10.clone.1 | convolution fusion | flops 547356672 | bytes 10231812 | tf_op jit(solution)/shard_map/while/body/eval_jaxpr/bkgt,ktd->bkgd/dot_general | solution.py:19
  135.5 0.7 reshape.162
  136.2 7.7 %all-to-all-start = ((f32[32,1,128]{2,1,0:T(1,128)}), f32[32,1,128]{2,1,0:T(1,128)S(1)}, u32[]{:S(2)}, u32[]{:S(2)}) async-start(f32[32,1,128]{2,1,0:T(1,128)} %reshape.162), calls=%async_computation | async-start | bytes 32768 | tf_op jit(solution)/shard_map/all_to_all | solution.py:88
  144.0 0.7 reshape.164
  144.7 7.7 %all-to-all-done = f32[32,1,128]{2,1,0:T(1,128)S(1)} async-done(((f32[32,1,128]{2,1,0:T(1,128)}), f32[32,1,128]{2,1,0:T(1,128)S(1)}, u32[]{:S(2)}, u32[]{:S(2)}) %all-to-all-start) | async-done | bytes 16416 | tf_op jit(solution)/shard_map/all_to_all | solution.py:88
  152.4 4.9 %all-to-all-start.2 = ((f32[32,1,128]{2,1,0:T(1,128)}), f32[32,1,128]{2,1,0:T(1,128)S(1)}, u32[]{:S(2)}, u32[]{:S(2)}) async-start(f32[32,1,128]{2,1,0:T(1,128)} %reshape.164), calls=%async_computation.2 | async-start | bytes 32768 | tf_op jit(solution)/shard_map/all_to_all | solution.py:95
  157.3 3.2 copy.60
  160.5 5.5 %all-to-all-done.2 = f32[32,1,128]{2,1,0:T(1,128)S(1)} async-done(((f32[32,1,128]{2,1,0:T(1,128)}), f32[32,1,128]{2,1,0:T(1,128)S(1)}, u32[]{:S(2)}, u32[]{:S(2)}) %all-to-all-start.2) | async-done | bytes 16416 | tf_op jit(solution)/shard_map/all_to_all | solution.py:95
  166.0 5.1 %all-to-all-start.1 = ((f32[32,32,4,128]{3,1,2,0:T(8,128)}), f32[32,32,4,128]{3,1,2,0:T(8,128)S(1)}, u32[]{:S(2)}, u32[]{:S(2)}) async-start(f32[32,32,4,128]{3,1,2,0:T(8,128)} %copy.60), calls=%async_computation.1 | async-start | bytes 4194304 | tf_op jit(solution)/shard_map/all_to_all | solution.py:102
  171.3 0.7 fusion.34
  172.1 0.9 fusion.27
  175.6 0.7 reshape.165
  176.4 0.9 multiply_reduce_fusion.1
  177.3 0.7 multiply_add_fusion
  178.0 0.7 copy.67
  179.4 33.1 %all-to-all-done.1 = f32[32,32,4,128]{3,1,2,0:T(8,128)S(1)} async-done(((f32[32,32,4,128]{3,1,2,0:T(8,128)}), f32[32,32,4,128]{3,1,2,0:T(8,128)S(1)}, u32[]{:S(2)}, u32[]{:S(2)}) %all-to-all-start.1) | async-done | bytes 2097184 | tf_op jit(solution)/shard_map/all_to_all | solution.py:102
  213.2 1.7 fusion.24
  215.6 79.8 %all-gather.5.cloned.1.call-done = bf16[1024,512]{1,0:T(8,128)(2,1)} async-done(((bf16[32,512]{1,0:T(8,128)(2,1)}), bf16[1024,512]{1,0:T(8,128)(2,1)}) %all-gather.5.cloned.1.call-update) | async-done | bytes 1048592 | tf_op jit(solution)/shard_map/all_gather | solution.py:122
  295.4 2.6 fusion.35
  298.1 60.2 %reduce-scatter.2.cloned.1.call-done = f32[64,256]{1,0:T(8,128)} async-done(((f32[1024,256]{1,0:T(8,128)}), f32[64,256]{1,0:T(8,128)}) %reduce-scatter.2.cloned.1.call-update) | async-done | bytes 65552 | tf_op jit(solution)/shard_map/reduce_scatter | solution.py:123
  358.3 1.5 convert_element_type.19
  (60 shorter events, 7.5 us)
Async XLA Ops:
  6.5 164.8 %copy-start = (bf16[1,32,128,128]{3,2,1,0:T(8,128)(2,1)S(1)}, bf16[1,32,128,128]{3,2,1,0:T(8,128)(2,1)}, u32[]{:S(2)}) copy-start(bf16[1,32,128,128]{3,2,1,0:T(8,128)(2,1)} %param.17) | copy-start | bytes 3145732
  6.5 88.9 %all-gather.3.cloned.1.call-start = ((), (), s32[]{:S(2)}) async-start(), calls=%async_computation.4 | async-start | bytes 1081344 | tf_op jit(solution)/shard_map/all_gather | solution.py:57
  97.2 11.3 %copy-start.7 = (bf16[1,1024,128]{2,1,0:T(8,128)(2,1)S(1)}, bf16[1,1024,128]{2,1,0:T(8,128)(2,1)}, u32[]{:S(2)}) copy-start(bf16[1,1024,128]{2,1,0:T(8,128)(2,1)} %get-tuple-element.228) | copy-start | bytes 786436 | tf_op jit(solution)/shard_map/while
  117.2 11.3 %copy-start.7 = (bf16[1,1024,128]{2,1,0:T(8,128)(2,1)S(1)}, bf16[1,1024,128]{2,1,0:T(8,128)(2,1)}, u32[]{:S(2)}) copy-start(bf16[1,1024,128]{2,1,0:T(8,128)(2,1)} %get-tuple-element.228) | copy-start | bytes 786436 | tf_op jit(solution)/shard_map/while
  135.3 35.8 %copy-start.3 = (bf16[32,512]{1,0:T(8,128)(2,1)S(1)}, bf16[32,512]{1,0:T(8,128)(2,1)}, u32[]{:S(2)}) copy-start(bf16[32,512]{1,0:T(8,128)(2,1)} %param.11) | copy-start | bytes 98308
  135.3 35.9 %copy-start.6 = (s32[32]{0:T(128)S(1)}, s32[32]{0:T(128)}, u32[]{:S(2)}) copy-start(s32[32]{0:T(128)} %param.14) | copy-start | bytes 388
  135.3 160.1 %copy-start.1 = (bf16[512,256]{1,0:T(8,128)(2,1)S(1)}, bf16[512,256]{1,0:T(8,128)(2,1)}, u32[]{:S(2)}) copy-start(bf16[512,256]{1,0:T(8,128)(2,1)} %param.19) | copy-start | bytes 786436
  136.2 16.2 %all-to-all-start = ((f32[32,1,128]{2,1,0:T(1,128)}), f32[32,1,128]{2,1,0:T(1,128)S(1)}, u32[]{:S(2)}, u32[]{:S(2)}) async-start(f32[32,1,128]{2,1,0:T(1,128)} %reshape.162), calls=%async_computation | async-start | bytes 32768 | tf_op jit(solution)/shard_map/all_to_all | solution.py:88
  152.4 13.6 %all-to-all-start.2 = ((f32[32,1,128]{2,1,0:T(1,128)}), f32[32,1,128]{2,1,0:T(1,128)S(1)}, u32[]{:S(2)}, u32[]{:S(2)}) async-start(f32[32,1,128]{2,1,0:T(1,128)} %reshape.164), calls=%async_computation.2 | async-start | bytes 32768 | tf_op jit(solution)/shard_map/all_to_all | solution.py:95
  166.0 46.5 %all-to-all-start.1 = ((f32[32,32,4,128]{3,1,2,0:T(8,128)}), f32[32,32,4,128]{3,1,2,0:T(8,128)S(1)}, u32[]{:S(2)}, u32[]{:S(2)}) async-start(f32[32,32,4,128]{3,1,2,0:T(8,128)} %copy.60), calls=%async_computation.1 | async-start | bytes 4194304 | tf_op jit(solution)/shard_map/all_to_all | solution.py:102
  171.1 124.3 %all-gather.5.cloned.1.call-start = ((), (), s32[]{:S(2)}) async-start(), calls=%async_computation.5 | async-start | bytes 1081344 | tf_op jit(solution)/shard_map/all_gather | solution.py:122
  171.3 0.7 copy-start.4
  172.0 2.2 copy-start.2
  172.1 4.3 %copy-start.5 = (f32[32,4]{0,1:T(4,128)}, f32[32,4]{0,1:T(4,128)S(1)}, u32[]{:S(2)}) copy-start(f32[32,4]{0,1:T(4,128)S(1)} %copy.57) | copy-start | bytes 1540
  215.6 142.7 %reduce-scatter.2.cloned.1.call-start = ((), (), s32[]{:S(2)}) async-start(), calls=%async_computation.6 | async-start | bytes 1114112 | tf_op jit(solution)/shard_map/reduce_scatter | solution.py:123
Sparse Core Ops, SparseCore 0:
  10.5 84.8 all-gather.2
  215.7 79.6 all-gather.4
  298.2 60.0 reduce-scatter.1
where the time goes:
time: 367 us; the launch traced here: 366 us
  waiting for transfers between devices  274 us (75%)
  matrix products  30.8 us (8%)
  starting transfers between devices  17.8 us (5%)
  other arithmetic  17.7 us (5%)
  between operations  13.3 us (4%)
  local copies, waits for them, and re-layouts  12.8 us (3%)
    all_gather x1, waiting for transfers between devices, on_device(): gathered = lax.all_gather(queries, 'pool', axis=0, tiled=True)  86.8 us
    all_gather x1, waiting for transfers between devices, on_device(): everything = lax.all_gather(attention, 'pool', axis=0, tiled=True)  79.8 us
    reduce_scatter x1, waiting for transfers between devices, on_device(): lax.psum_scatter(jnp.dot(everything, out_weight, preferred_element_type=j...  60.2 us
    all_to_all x1, waiting for transfers between devices, on_device(): lax.all_to_all(owner_numer.reshape(pool_size, home_rows, local_heads, hea...  33.1 us
    dot_general x3, matrix products, soft_partial(): jnp.einsum(form, weights.astype(jnp.bfloat16), values, preferred_element_...  15.5 us
    dot_general x2, matrix products, owner_block(): jnp.einsum('bkgd,ktd->bkgt', query_block, prefix_keys, preferred_element_...  12 us
    reduce_sum x3, other arithmetic, soft_partial(): totals = jnp.sum(weights, axis=-1)  11.1 us
    all_to_all x1, waiting for transfers between devices, on_device(): lax.all_to_all(owner_high.reshape(pool_size, home_rows, local_heads), 'po...  7.69 us
  transfers between devices with their start and end apart: 6, of which 6 were waited for; matrix products, arithmetic and copies ran while one was open for 4% of the time, Pallas kernels for 0%

commit v1 on v0

v1 whole, which is shorter than its diff:
```python
import math

import jax
import jax.numpy as jnp
from jax import lax
from jax.experimental import pallas as pl
from jax.experimental.pallas import tpu as pltpu
from jax.sharding import PartitionSpec as P

CPP = 16
NX, NY = 4, 8
HEADS = 4
HD = 128
ROWS = 32
MEMBERS = 16
LANES = 128
TAB = 16
HIDE = -1e30
FLOOR = -262144.0
LOG2E = 1.4426950408889634
SCALE = LOG2E / math.sqrt(HD)
f32, bf16 = jnp.float32, jnp.bfloat16

GROUP_X = ((0, 3), (1, 2))
GROUPS = [[x * NY + y for x in xs for y in range(NY)] for xs in GROUP_X]
PAIR = [(x * NY + y, (x ^ 1) * NY + y) for x in range(NX) for y in range(NY)]


def nt_dot(a, b):
    return lax.dot_general(a, b, (((1,), (1,)), ((), ())), preferred_element_type=f32)


def suffix_kernel(q_ref, len_ref, k_ref, v_ref, numer_ref, stat_ref):
    rows = HEADS * ROWS
    q = jnp.concatenate([q_ref[:, j * HD : (j + 1) * HD] for j in range(HEADS)], axis=0)
    row = lax.broadcasted_iota(jnp.int32, (rows, LANES), 0) % ROWS
    lane = lax.broadcasted_iota(jnp.int32, (rows, LANES), 1)
    live = lane < jnp.concatenate([len_ref[...]] * HEADS, axis=0)
    picked = jnp.full((rows, LANES), HIDE, f32)
    for b in range(ROWS):
        picked = jnp.where(row == b, nt_dot(q, k_ref[b]), picked)
    picked = jnp.where(live, picked, HIDE)
    high = jnp.max(picked, axis=1, keepdims=True)
    weights = jnp.exp2((picked - high) * SCALE)
    totals = jnp.sum(weights, axis=1, keepdims=True)
    rounded = weights.astype(bf16)
    zero = jnp.zeros((rows, LANES), bf16)
    acc = jnp.zeros((rows, HD), f32)
    for b in range(0, ROWS, 2):
        w = jnp.concatenate(
            [jnp.where(row == b, weights, 0.0).astype(bf16), jnp.where(row == b + 1, weights, 0.0).astype(bf16)],
            axis=1,
        )
        v = jnp.concatenate([v_ref[b], v_ref[b + 1]], axis=0)
        acc = acc + jnp.dot(w, v, preferred_element_type=f32)
    for j in range(HEADS):
        numer_ref[:, j * HD : (j + 1) * HD] = acc[j * ROWS : (j + 1) * ROWS]
    lane = lax.broadcasted_iota(jnp.int32, (ROWS, LANES), 1)
    stat = jnp.zeros((ROWS, LANES), f32)
    for j in range(HEADS):
        part = slice(j * ROWS, (j + 1) * ROWS)
        stat = jnp.where(lane == j, high[part] * SCALE, stat)
        stat = jnp.where(lane == HEADS + j, totals[part], stat)
    stat_ref[...] = stat


def owner_kernel(q_ref, hide_ref, own_ref, oth_ref, out_ref, keys_ref):
    tokens = (own_ref.shape[0] - TAB) // 2
    slots = tokens // LANES
    lane = lax.broadcasted_iota(jnp.int32, (LANES, LANES), 1)
    for o, ref in enumerate((own_ref, oth_ref)):
        table = ref[2 * tokens : 2 * tokens + TAB, :].astype(f32)
        keys_ref[o, :, :HD] = ref[:tokens, :]
        for s in range(slots):
            other = (lane < CPP) & (lane.astype(f32) != table[0:1, s : s + 1])
            keys_ref[o, s * LANES : (s + 1) * LANES, HD:] = jnp.where(other, 1.0, 0.0).astype(bf16)
    branches = MEMBERS * ROWS
    block = 256
    lane = lax.broadcasted_iota(jnp.int32, (block, LANES), 1)
    per = block // ROWS
    for r in range(branches // block):
        hide = hide_ref[r * block : (r + 1) * block, :]
        stat = jnp.zeros((block, LANES), f32)
        for j in range(HEADS):
            q = q_ref[r * per : (r + 1) * per, :, j * HD : (j + 1) * HD].reshape(block, HD)
            q = jnp.concatenate([q, hide], axis=1)
            parts = []
            for o, ref in enumerate((own_ref, oth_ref)):
                scores = nt_dot(q, keys_ref[o])
                high = jnp.maximum(jnp.max(scores, axis=1, keepdims=True), FLOOR)
                weights = jnp.exp2((scores - high) * SCALE)
                totals = jnp.sum(weights, axis=1, keepdims=True)
                numer = jnp.dot(weights.astype(bf16), ref[tokens : 2 * tokens, :], preferred_element_type=f32)
                parts.append((high * SCALE, totals, numer))
            (ha, ta, na), (hb, tb, nb) = parts
            high = jnp.maximum(ha, hb).astype(bf16).astype(f32)
            fa, fb = jnp.exp2(ha - high), jnp.exp2(hb - high)
            numer = na * fa + nb * fb
            totals = ta * fa + tb * fb
            coarse = totals.astype(bf16).astype(f32)
            out_ref[r * per : (r + 1) * per, :, j * HD : (j + 1) * HD] = numer.astype(bf16).reshape(per, ROWS, HD)
            stat = jnp.where(lane == j, high, stat)
            stat = jnp.where(lane == HEADS + j, coarse, stat)
            stat = jnp.where(lane == 2 * HEADS + j, totals - coarse, stat)
        out_ref[r * per : (r + 1) * per, :, HEADS * HD :] = stat.astype(bf16).reshape(per, ROWS, LANES)


def join_kernel(got_ref, numer_ref, stat_ref, out_ref):
    wide = HEADS * HD
    own = stat_ref[...]
    top = own
    for i in range(MEMBERS):
        top = jnp.maximum(top, got_ref[i, :, wide:].astype(f32))
    lane = lax.broadcasted_iota(jnp.int32, (ROWS, LANES), 1)
    shift = lane < HEADS
    top = jnp.where(shift, top, 0.0)
    fac_own = jnp.exp2(jnp.where(shift, own, 0.0) - top)
    numer = [numer_ref[:, j * HD : (j + 1) * HD] * fac_own[:, j : j + 1] for j in range(HEADS)]
    total = [own[:, HEADS + j : HEADS + j + 1] * fac_own[:, j : j + 1] for j in range(HEADS)]
    for i in range(MEMBERS):
        stat = got_ref[i, :, wide:].astype(f32)
        fac = jnp.exp2(jnp.where(shift, stat, 0.0) - top)
        for j in range(HEADS):
            f = fac[:, j : j + 1]
            numer[j] = numer[j] + got_ref[i, :, j * HD : (j + 1) * HD].astype(f32) * f
            t = stat[:, HEADS + j : HEADS + j + 1] + stat[:, 2 * HEADS + j : 2 * HEADS + j + 1]
            total[j] = total[j] + t * f
    for j in range(HEADS):
        out_ref[:, j * HD : (j + 1) * HD] = (numer[j] / total[j]).astype(bf16)


def project_kernel(att_ref, w_ref, out_ref):
    depth = att_ref.shape[2]
    half = att_ref.shape[0] // 2
    acc = jnp.zeros(out_ref.shape, f32)
    for h in range(half):
        rows = jnp.concatenate([att_ref[h], att_ref[half + h]], axis=0)
        acc = acc + jnp.dot(rows, w_ref[h * depth : (h + 1) * depth, :], preferred_element_type=f32)
    out_ref[...] = acc.astype(bf16)


def call(kernel, out_shape, *args, flops=0, moved=0, scratch=()):
    return pl.pallas_call(
        kernel,
        out_shape=out_shape,
        scratch_shapes=scratch,
        compiler_params=pltpu.CompilerParams(vmem_limit_bytes=40 * 2**20),
        cost_estimate=pl.CostEstimate(flops=flops, bytes_accessed=moved, transcendentals=0),
    )(*args)


def on_device(
    queries,
    branch_prefix,
    stretch_table,
    suffix_len,
    prefix_keys,
    prefix_values,
    suffix_keys,
    suffix_values,
    out_weight,
):
    pool = lax.axis_index("pool")
    x = pool // NY
    slots = stretch_table.shape[0]

    prefixes = (stretch_table // CPP).astype(bf16)
    table = jnp.zeros((TAB, LANES), bf16).at[0, :slots].set(prefixes)
    own = jnp.concatenate([prefix_keys[0], prefix_values[0], table], axis=0)
    oth = lax.ppermute(own, "pool", PAIR)

    weight = lax.all_gather(out_weight, "head", axis=0, tiled=True)

    got = lax.all_to_all(
        jnp.broadcast_to(queries[None], (MEMBERS,) + queries.shape),
        "pool",
        split_axis=0,
        concat_axis=0,
        tiled=True,
        axis_index_groups=GROUPS,
    )
    span = NY * ROWS
    outer = (x == GROUP_X[0][0]) | (x == GROUP_X[0][1])
    mine = jnp.where(
        outer,
        jnp.concatenate([branch_prefix[xx * span : (xx + 1) * span] for xx in GROUP_X[0]]),
        jnp.concatenate([branch_prefix[xx * span : (xx + 1) * span] for xx in GROUP_X[1]]),
    )
    hide = jnp.where(mine[:, None] == jnp.arange(LANES, dtype=jnp.int32)[None, :], HIDE, 0.0).astype(bf16)

    suffix_numer, suffix_stat = call(
        suffix_kernel,
        (
            jax.ShapeDtypeStruct((ROWS, HEADS * HD), f32),
            jax.ShapeDtypeStruct((ROWS, LANES), f32),
        ),
        queries,
        suffix_len[:, None],
        suffix_keys[0],
        suffix_values[0],
        flops=2 * 2 * 128 * 128 * 4096,
        moved=2 * 2**20,
    )

    state = call(
        owner_kernel,
        jax.ShapeDtypeStruct((MEMBERS, ROWS, HEADS * HD + LANES), bf16),
        got,
        hide,
        own,
        oth,
        flops=4 * 2048 * 2048 * 128,
        moved=2 * 2**20,
        scratch=[pltpu.VMEM((2, prefix_keys.shape[1], 2 * HD), bf16)],
    )
    state = lax.all_to_all(
        state, "pool", split_axis=0, concat_axis=0, tiled=True, axis_index_groups=GROUPS
    )
    attention = call(
        join_kernel,
        jax.ShapeDtypeStruct((ROWS, HEADS * HD), bf16),
        state,
        suffix_numer,
        suffix_stat,
        flops=2**21,
        moved=2**20,
    )

    heads = lax.axis_size("head")
    moves = [
        (p * heads + h, ((p % 2) * heads + h) * heads + p // 2)
        for p in range(NX * NY)
        for h in range(heads)
    ]
    attention = lax.ppermute(attention, ("pool", "head"), moves)
    everything = lax.all_to_all(
        jnp.broadcast_to(attention[None], (NX * NY,) + attention.shape),
        "pool",
        split_axis=0,
        concat_axis=0,
        tiled=True,
    )
    return call(
        project_kernel,
        jax.ShapeDtypeStruct((2 * ROWS, out_weight.shape[1]), bf16),
        everything,
        weight,
        flops=2 * 64 * 8192 * 256,
        moved=5 * 2**20,
    )


def solution(mesh):
    in_specs = (
        P("pool", "head"),
        P(),
        P("pool"),
        P("pool"),
        P("head", "pool", None),
        P("head", "pool", None),
        P("head", "pool", None, None),
        P("head", "pool", None, None),
        P("head", "pool"),
    )
    out_specs = P("head", "pool")
    return jax.shard_map(
        on_device, mesh=mesh, in_specs=in_specs, out_specs=out_specs, check_vma=False
    )
```

time: 367 us -> 132 us (0.36)
  the two profiles are of different devices: /device:TPU:2 before, /device:TPU:8 now
where the time goes in v1:
time: 132 us
  blocking collectives  45.1 us (34%)
  waiting for transfers between devices  34.2 us (26%)
  starting transfers between devices  22.5 us (17%)
  between operations  13.5 us (10%)
  Pallas kernels  12.2 us (9%)
  local copies, waits for them, and re-layouts  4.02 us (3%)
    all_to_all x1, blocking collectives, on_device(): lax.all_to_all(jnp.broadcast_to(attention[None], (NX * NY,) + attention.s...  45.1 us
    all_to_all x1, waiting for transfers between devices, on_device(): lax.all_to_all(state, 'pool', split_axis=0, concat_axis=0, tiled=True, ax...  16.5 us
    ppermute x1, waiting for transfers between devices, on_device(): oth = lax.ppermute(own, 'pool', PAIR)  12.7 us
    pallas_call x4, Pallas kernels, call(): pl.pallas_call(kernel, out_shape=out_shape, scratch_shapes=scratch, compi...  12.2 us
    all_to_all x1, starting transfers between devices, on_device(): lax.all_to_all(jnp.broadcast_to(queries[None], (MEMBERS,) + queries.shape...  9.89 us
    all_to_all x1, starting transfers between devices, on_device(): lax.all_to_all(state, 'pool', split_axis=0, concat_axis=0, tiled=True, ax...  8.57 us
    ppermute x1, waiting for transfers between devices, on_device(): attention = lax.ppermute(attention, ('pool', 'head'), moves)  3.32 us
  transfers between devices with their start and end apart: 5, of which 4 were waited for; matrix products, arithmetic and copies ran while one was open for 2% of the time, Pallas kernels for 8%

profile of v1, /device:TPU:8, one launch (start us, length us, event | category | flops | bytes accessed | tf_op | source)
XLA Modules:
  0.0 131.7 jit_solution(12674512469335078022)
XLA Ops:
  6.5 0.0 copy-start.8
  6.5 0.0 copy-start.5
  6.5 0.0 copy-start.4
  6.5 0.0 all-gather.2.cloned.1.call-start
  6.5 0.7 all-gather.2.cloned.1.call-update
  7.3 1.6 %broadcast_in_dim.14 = bf16[16,32,512]{2,1,0:T(8,128)(2,1)} broadcast(bf16[32,512]{1,0:T(8,128)(2,1)} %q_ref.1), dimensions={1,2} | broadcast | bytes 557056 | tf_op jit(solution)/shard_map/broadcast_in_dim | solution.py:175
  8.9 0.0 copy-start.6
  8.9 9.9 %all-to-all-start = ((bf16[16,32,512]{2,1,0:T(8,128)(2,1)}), bf16[16,32,512]{2,1,0:T(8,128)(2,1)S(1)}, u32[]{:S(2)}, u32[]{:S(2)}) async-start(bf16[16,32,512]{2,1,0:T(8,128)(2,1)} %broadcast_in_dim.14), calls=%async_computation | async-start | bytes 1048576 | tf_op jit(solution)/shard_map/all_to_all | solution.py:174
  18.8 0.0 copy-done.8
  18.8 0.0 copy-done.5
  18.8 0.0 copy-done.4
  18.8 2.1 %collective-permute-start = (bf16[2064,128]{1,0:T(8,128)(2,1)S(1)}, bf16[2064,128]{1,0:T(8,128)(2,1)S(1)}, u32[]{:S(2)}, u32[]{:S(2)}) collective-permute-start(bf16[2064,128]{1,0:T(8,128)(2,1)S(1)} %fusion.1.own_ref), channel_id=1, source_target_pairs={{0,128},{16,144},{32,160},{48,176},{64,192},{80,208},{96,224},{112... | collective-permute-start | bytes 1585160 | tf_op jit(solution)/shard_map/ppermute | solution.py:170
  21.0 0.0 copy-done.6
  21.0 0.1 select_convert_fusion.hide_ref
  21.2 12.7 %collective-permute-done.oth_ref = bf16[2064,128]{1,0:T(8,128)(2,1)S(1)} collective-permute-done((bf16[2064,128]{1,0:T(8,128)(2,1)S(1)}, bf16[2064,128]{1,0:T(8,128)(2,1)S(1)}, u32[]{:S(2)}, u32[]{:S(2)}) %collective-permute-start) | collective-permute-done | bytes 528416 | tf_op jit(solution)/shard_map/ppermute | solution.py:170
  33.9 0.9 all-to-all-done.q_ref
  34.8 8.9 %shard_map.91 = bf16[16,32,640]{2,1,0:T(8,128)(2,1)} custom-call(bf16[16,32,512]{2,1,0:T(8,128)(2,1)S(1)} %all-to-all-done.q_ref, bf16[512,128]{1,0:T(8,128)(2,1)S(1)} %select_convert_fusion.hide_ref, bf16[2064,128]{1,0:T(8,128)(2,1)S(1)} %fusion.1.own_ref, bf16[2064,128]{1,0:T(8,128)(2,1)S(1)} %collective-permute-done.oth_ref), custom_call_target="tpu_custom_call" | custom-call | flops 2147483648 | bytes 2097152 | tf_op jit(solution)/shard_map/pallas_call | solution.py:143
  43.8 8.6 %all-to-all-start.1 = ((bf16[16,32,640]{2,1,0:T(8,128)(2,1)}), bf16[16,32,640]{2,1,0:T(8,128)(2,1)S(1)}, u32[]{:S(2)}, u32[]{:S(2)}) async-start(bf16[16,32,640]{2,1,0:T(8,128)(2,1)} %shard_map.91), calls=%async_computation.1 | async-start | bytes 1310720 | tf_op jit(solution)/shard_map/all_to_all | solution.py:216
  52.3 0.0 copy-done.7
  52.3 0.1 copy.10.len_ref
  52.4 0.0 copy-done.2
  52.4 0.0 copy-done.1
  52.4 0.0 copy-done.3
  52.4 1.1 shard_map.92
  53.6 16.5 %all-to-all-done.1.got_ref = bf16[16,32,640]{2,1,0:T(8,128)(2,1)S(1)} async-done(((bf16[16,32,640]{2,1,0:T(8,128)(2,1)}), bf16[16,32,640]{2,1,0:T(8,128)(2,1)S(1)}, u32[]{:S(2)}, u32[]{:S(2)}) %all-to-all-start.1) | async-done | bytes 655392 | tf_op jit(solution)/shard_map/all_to_all | solution.py:216
  70.1 0.7 shard_map.93
  70.8 1.9 %collective-permute-start.1 = (bf16[32,512]{1,0:T(8,128)(2,1)S(1)}, bf16[32,512]{1,0:T(8,128)(2,1)S(1)}, u32[]{:S(2)}, u32[]{:S(2)}) collective-permute-start(bf16[32,512]{1,0:T(8,128)(2,1)S(1)} %shard_map.93), channel_id=1, source_target_pairs={{0,0},{1,16},{2,32},{3,48},{4,64},{5,80},{6,96},{7,112},{8,128},{9... | collective-permute-start | bytes 98312 | tf_op jit(solution)/shard_map/ppermute | solution.py:235
  72.7 3.3 %collective-permute-done.1 = bf16[32,512]{1,0:T(8,128)(2,1)S(1)} collective-permute-done((bf16[32,512]{1,0:T(8,128)(2,1)S(1)}, bf16[32,512]{1,0:T(8,128)(2,1)S(1)}, u32[]{:S(2)}, u32[]{:S(2)}) %collective-permute-start.1) | collective-permute-done | bytes 32800 | tf_op jit(solution)/shard_map/ppermute | solution.py:235
  76.1 0.1 broadcast_in_dim.30
  76.2 45.1 %all_to_all.15.att_ref = bf16[32,32,512]{2,1,0:T(8,128)(2,1)S(1)} all-to-all(bf16[32,32,512]{2,1,0:T(8,128)(2,1)S(1)} %broadcast_in_dim.30), channel_id=1, replica_groups=mesh['pool'=32,'head'=16] {'pool'}, dimensions={0} | all-to-all | bytes 2097152 | tf_op jit(solution)/shard_map/all_to_all | solution.py:236
  121.2 2.2 %copy-done = bf16[8192,256]{1,0:T(8,128)(2,1)S(1)} copy-done((bf16[8192,256]{1,0:T(8,128)(2,1)S(1)}, bf16[8192,256]{1,0:T(8,128)(2,1)}, u32[]{:S(2)}) %copy-start) | copy-done | bytes 4194328
  123.4 1.5 %shard_map.94 = bf16[64,256]{1,0:T(8,128)(2,1)} custom-call(bf16[32,32,512]{2,1,0:T(8,128)(2,1)S(1)} %all_to_all.15.att_ref, bf16[8192,256]{1,0:T(8,128)(2,1)S(1)} %copy-done), custom_call_target="tpu_custom_call" | custom-call | flops 268435456 | bytes 5242880 | tf_op jit(solution)/shard_map/pallas_call | solution.py:143
  (10 shorter events, 0.1 us)
Async XLA Ops:
  6.5 12.2 %copy-start.8 = (s32[8]{0:T(128)S(1)}, s32[8]{0:T(128)}, u32[]{:S(2)}) copy-start(s32[8]{0:T(128)} %param.13) | copy-start | bytes 100
  6.5 12.2 %copy-start.5 = (bf16[1,1024,128]{2,1,0:T(8,128)(2,1)S(1)}, bf16[1,1024,128]{2,1,0:T(8,128)(2,1)}, u32[]{:S(2)}) copy-start(bf16[1,1024,128]{2,1,0:T(8,128)(2,1)} %param.15) | copy-start | bytes 786436
  6.5 12.2 %copy-start.4 = (bf16[1,1024,128]{2,1,0:T(8,128)(2,1)S(1)}, bf16[1,1024,128]{2,1,0:T(8,128)(2,1)}, u32[]{:S(2)}) copy-start(bf16[1,1024,128]{2,1,0:T(8,128)(2,1)} %param.16) | copy-start | bytes 786436
  6.5 114.7 %all-gather.2.cloned.1.call-start = ((), (), s32[]{:S(2)}) async-start(), calls=%async_computation.3 | async-start | bytes 4456448 | tf_op jit(solution)/shard_map/all_gather | solution.py:172
  8.9 12.1 %copy-start.6 = (s32[1024]{0:T(1024)S(1)}, s32[1024]{0:T(1024)}, u32[]{:S(2)}) copy-start(s32[1024]{0:T(1024)} %param.12) | copy-start | bytes 12292
  8.9 26.0 %all-to-all-start = ((bf16[16,32,512]{2,1,0:T(8,128)(2,1)}), bf16[16,32,512]{2,1,0:T(8,128)(2,1)S(1)}, u32[]{:S(2)}, u32[]{:S(2)}) async-start(bf16[16,32,512]{2,1,0:T(8,128)(2,1)} %broadcast_in_dim.14), calls=%async_computation | async-start | bytes 1048576 | tf_op jit(solution)/shard_map/all_to_all | solution.py:174
  18.8 15.1 %collective-permute-start = (bf16[2064,128]{1,0:T(8,128)(2,1)S(1)}, bf16[2064,128]{1,0:T(8,128)(2,1)S(1)}, u32[]{:S(2)}, u32[]{:S(2)}) collective-permute-start(bf16[2064,128]{1,0:T(8,128)(2,1)S(1)} %fusion.1.own_ref), channel_id=1, source_target_pairs={{0,128},{16,144},{32,160},{48,176},{64,192},{80,208},{96,224},{112... | collective-permute-start | bytes 1585160 | tf_op jit(solution)/shard_map/ppermute | solution.py:170
  34.8 17.6 %copy-start.2 = (bf16[1,32,128,128]{3,2,1,0:T(8,128)(2,1)S(1)}, bf16[1,32,128,128]{3,2,1,0:T(8,128)(2,1)}, u32[]{:S(2)}) copy-start(bf16[1,32,128,128]{3,2,1,0:T(8,128)(2,1)} %param.18) | copy-start | bytes 3145732
  43.8 8.6 %copy-start.7 = (s32[32]{0:T(128)S(1)}, s32[32]{0:T(128)}, u32[]{:S(2)}) copy-start(s32[32]{0:T(128)} %param.14) | copy-start | bytes 388
  43.8 8.7 %copy-start.1 = (bf16[1,32,128,128]{3,2,1,0:T(8,128)(2,1)S(1)}, bf16[1,32,128,128]{3,2,1,0:T(8,128)(2,1)}, u32[]{:S(2)}) copy-start(bf16[1,32,128,128]{3,2,1,0:T(8,128)(2,1)} %param.17) | copy-start | bytes 3145732
  43.8 8.7 %copy-start.3 = (bf16[32,512]{1,0:T(8,128)(2,1)S(1)}, bf16[32,512]{1,0:T(8,128)(2,1)}, u32[]{:S(2)}) copy-start(bf16[32,512]{1,0:T(8,128)(2,1)} %q_ref.1) | copy-start | bytes 98308
  43.8 26.3 %all-to-all-start.1 = ((bf16[16,32,640]{2,1,0:T(8,128)(2,1)}), bf16[16,32,640]{2,1,0:T(8,128)(2,1)S(1)}, u32[]{:S(2)}, u32[]{:S(2)}) async-start(bf16[16,32,640]{2,1,0:T(8,128)(2,1)} %shard_map.91), calls=%async_computation.1 | async-start | bytes 1310720 | tf_op jit(solution)/shard_map/all_to_all | solution.py:216
  70.8 5.2 %collective-permute-start.1 = (bf16[32,512]{1,0:T(8,128)(2,1)S(1)}, bf16[32,512]{1,0:T(8,128)(2,1)S(1)}, u32[]{:S(2)}, u32[]{:S(2)}) collective-permute-start(bf16[32,512]{1,0:T(8,128)(2,1)S(1)} %shard_map.93), channel_id=1, source_target_pairs={{0,0},{1,16},{2,32},{3,48},{4,64},{5,80},{6,96},{7,112},{8,128},{9... | collective-permute-start | bytes 98312 | tf_op jit(solution)/shard_map/ppermute | solution.py:235
  121.2 2.2 %copy-start = (bf16[8192,256]{1,0:T(8,128)(2,1)S(1)}, bf16[8192,256]{1,0:T(8,128)(2,1)}, u32[]{:S(2)}) copy-start(bf16[8192,256]{1,0:T(8,128)(2,1)} %all-gather.2.cloned.1.call-done.w_ref) | copy-start | bytes 12582916
Sparse Core Ops, SparseCore 0:
  9.5 50.2 all-gather.1

commit v2 on v1

--- a/solution.py
+++ b/solution.py
@@ -24,6 +24,20 @@
 GROUP_X = ((0, 3), (1, 2))
 GROUPS = [[x * NY + y for x in xs for y in range(NY)] for xs in GROUP_X]
 PAIR = [(x * NY + y, (x ^ 1) * NY + y) for x in range(NX) for y in range(NY)]
+X_GROUPS = [[x * NY + y for x in range(NX)] for y in range(NY)]
+Y_GROUPS = [[x * NY + y for y in range(NY)] for x in range(NX)]
+NH = 16
+
+
+def place(x, y, h):
+    return (x * NY + y) * NH + h
+
+
+EVERY = [(x, y, h) for x in range(NX) for y in range(NY) for h in range(NH)]
+WEIGHT_MOVES = [(place(x, y, h), place(h % NX, y, h - h % NX + x)) for x, y, h in EVERY]
+ATTENTION_MOVES = [
+    (place(x, y, h), place(h % NX, (y % 2) * NX + h // NX, NX * x + y // 2)) for x, y, h in EVERY
+]
 
 
 def nt_dot(a, b):
@@ -75,7 +89,7 @@
             other = (lane < CPP) & (lane.astype(f32) != table[0:1, s : s + 1])
             keys_ref[o, s * LANES : (s + 1) * LANES, HD:] = jnp.where(other, 1.0, 0.0).astype(bf16)
     branches = MEMBERS * ROWS
-    block = 256
+    block = 512
     lane = lax.broadcasted_iota(jnp.int32, (block, LANES), 1)
     per = block // ROWS
     for r in range(branches // block):
@@ -132,10 +146,19 @@
 def project_kernel(att_ref, w_ref, out_ref):
     depth = att_ref.shape[2]
     half = att_ref.shape[0] // 2
-    acc = jnp.zeros(out_ref.shape, f32)
-    for h in range(half):
-        rows = jnp.concatenate([att_ref[h], att_ref[half + h]], axis=0)
-        acc = acc + jnp.dot(rows, w_ref[h * depth : (h + 1) * depth, :], preferred_element_type=f32)
+    for c in range(out_ref.shape[0]):
+        acc = jnp.zeros(out_ref.shape[1:], f32)
+        for k in range(half):
+            rows = jnp.concatenate([att_ref[k], att_ref[half + k]], axis=0)
+            i = k * out_ref.shape[0] + c
+            acc = acc + jnp.dot(rows, w_ref[i * depth : (i + 1) * depth, :], preferred_element_type=f32)
+        out_ref[c] = acc.astype(out_ref.dtype)
+
+
+def sum_kernel(part_ref, out_ref):
+    acc = part_ref[0].astype(f32)
+    for c in range(1, part_ref.shape[0]):
+        acc = acc + part_ref[c].astype(f32)
     out_ref[...] = acc.astype(bf16)
 
 
@@ -147,6 +170,10 @@
         compiler_params=pltpu.CompilerParams(vmem_limit_bytes=40 * 2**20),
         cost_estimate=pl.CostEstimate(flops=flops, bytes_accessed=moved, transcendentals=0),
     )(*args)
+
+
+def after(value, other):
+    return lax.optimization_barrier((value, other))[0]
 
 
 def on_device(
@@ -169,8 +196,6 @@
     own = jnp.concatenate([prefix_keys[0], prefix_values[0], table], axis=0)
     oth = lax.ppermute(own, "pool", PAIR)
 
-    weight = lax.all_gather(out_weight, "head", axis=0, tiled=True)
-
     got = lax.all_to_all(
         jnp.broadcast_to(queries[None], (MEMBERS,) + queries.shape),
         "pool",
@@ -179,6 +204,9 @@
         tiled=True,
         axis_index_groups=GROUPS,
     )
+    weight = lax.ppermute(out_weight, ("pool", "head"), WEIGHT_MOVES)
+    got, oth, weight = lax.optimization_barrier((got, oth, weight))
+
     span = NY * ROWS
     outer = (x == GROUP_X[0][0]) | (x == GROUP_X[0][1])
     mine = jnp.where(
@@ -213,6 +241,7 @@
         moved=2 * 2**20,
         scratch=[pltpu.VMEM((2, prefix_keys.shape[1], 2 * HD), bf16)],
     )
+    weight = lax.all_gather(weight, "head", axis=0, tiled=True)
     state = lax.all_to_all(
         state, "pool", split_axis=0, concat_axis=0, tiled=True, axis_index_groups=GROUPS
     )
@@ -226,27 +255,32 @@
         moved=2**20,
     )
 
-    heads = lax.axis_size("head")
-    moves = [
-        (p * heads + h, ((p % 2) * heads + h) * heads + p // 2)
-        for p in range(NX * NY)
-        for h in range(heads)
-    ]
-    attention = lax.ppermute(attention, ("pool", "head"), moves)
-    everything = lax.all_to_all(
-        jnp.broadcast_to(attention[None], (NX * NY,) + attention.shape),
+    attention = lax.ppermute(attention, ("pool", "head"), ATTENTION_MOVES)
+    blocks = lax.all_to_all(
+        jnp.broadcast_to(attention[None], (NY,) + attention.shape),
         "pool",
         split_axis=0,
         concat_axis=0,
         tiled=True,
-    )
-    return call(
+        axis_index_groups=Y_GROUPS,
+    )
+    partial = call(
         project_kernel,
-        jax.ShapeDtypeStruct((2 * ROWS, out_weight.shape[1]), bf16),
-        everything,
+        jax.ShapeDtypeStruct((NX, 2 * ROWS, out_weight.shape[1]), bf16),
+        blocks,
         weight,
         flops=2 * 64 * 8192 * 256,
         moved=5 * 2**20,
+    )
+    partial = lax.all_to_all(
+        partial, "pool", split_axis=0, concat_axis=0, tiled=True, axis_index_groups=X_GROUPS
+    )
+    return call(
+        sum_kernel,
+        jax.ShapeDtypeStruct((2 * ROWS, out_weight.shape[1]), bf16),
+        partial,
+        flops=2**16,
+        moved=2**18,
     )
 
 

time: 132 us -> 124 us (0.939)
  the two profiles are of different devices: /device:TPU:8 before, /device:TPU:64 now
where the time goes in v2:
time: 124 us
  waiting for transfers between devices  32.1 us (26%)
  starting transfers between devices  31.9 us (26%)
  blocking collectives  30.7 us (25%)
  between operations  13.6 us (11%)
  Pallas kernels  10.7 us (9%)
  local copies, waits for them, and re-layouts  4.41 us (4%)
    all_to_all x1, blocking collectives, on_device(): lax.all_to_all(jnp.broadcast_to(attention[None], (NY,) + attention.shape)...  16.7 us
    all_to_all x1, blocking collectives, on_device(): lax.all_to_all(partial, 'pool', split_axis=0, concat_axis=0, tiled=True,...  14 us
    all_to_all x1, waiting for transfers between devices, on_device(): lax.all_to_all(state, 'pool', split_axis=0, concat_axis=0, tiled=True, ax...  13 us
    all_to_all x1, starting transfers between devices, on_device(): lax.all_to_all(state, 'pool', split_axis=0, concat_axis=0, tiled=True, ax...  12.9 us
    pallas_call x5, Pallas kernels, call(): pl.pallas_call(kernel, out_shape=out_shape, scratch_shapes=scratch, compi...  10.7 us
    ppermute x1, waiting for transfers between devices, on_device(): weight = lax.ppermute(out_weight, ('pool', 'head'), WEIGHT_MOVES)  9.77 us
    all_to_all x1, starting transfers between devices, on_device(): lax.all_to_all(jnp.broadcast_to(queries[None], (MEMBERS,) + queries.shape...  9.53 us
    ppermute x1, waiting for transfers between devices, on_device(): attention = lax.ppermute(attention, ('pool', 'head'), ATTENTION_MOVES)  9.04 us
  transfers between devices with their start and end apart: 6, of which 4 were waited for; matrix products, arithmetic and copies ran while one was open for 0% of the time, Pallas kernels for 7%

profile of v2, /device:TPU:64, one launch (start us, length us, event | category | flops | bytes accessed | tf_op | source)
XLA Modules:
  0.0 123.6 jit_solution(13642316472572487144)
XLA Ops:
  6.5 1.7 %broadcast_in_dim.14 = bf16[16,32,512]{2,1,0:T(8,128)(2,1)} broadcast(bf16[32,512]{1,0:T(8,128)(2,1)} %q_ref.1), dimensions={1,2} | broadcast | bytes 557056 | tf_op jit(solution)/shard_map/broadcast_in_dim | solution.py:200
  8.2 9.5 %all-to-all-start = ((bf16[16,32,512]{2,1,0:T(8,128)(2,1)}), bf16[16,32,512]{2,1,0:T(8,128)(2,1)S(1)}, u32[]{:S(2)}, u32[]{:S(2)}) async-start(bf16[16,32,512]{2,1,0:T(8,128)(2,1)} %broadcast_in_dim.14), calls=%async_computation | async-start | bytes 1048576 | tf_op jit(solution)/shard_map/all_to_all | solution.py:199
  17.8 0.0 all-gather.2.cloned.1.call-start
  17.8 0.0 copy-done.10
  17.8 0.0 copy-done.6
  17.8 0.0 copy-done.5
  17.9 2.1 %collective-permute-start = (bf16[2064,128]{1,0:T(8,128)(2,1)S(1)}, bf16[2064,128]{1,0:T(8,128)(2,1)S(1)}, u32[]{:S(2)}, u32[]{:S(2)}) collective-permute-start(bf16[2064,128]{1,0:T(8,128)(2,1)S(1)} %fusion.1.own_ref), channel_id=1, source_target_pairs={{0,128},{16,144},{32,160},{48,176},{64,192},{80,208},{96,224},{112... | collective-permute-start | bytes 1585160 | tf_op jit(solution)/shard_map/ppermute | solution.py:197
  20.0 0.0 copy-done.9
  20.0 5.4 %collective-permute-start.1 = (bf16[512,256]{1,0:T(8,128)(2,1)S(1)}, bf16[512,256]{1,0:T(8,128)(2,1)S(1)}, u32[]{:S(2)}, u32[]{:S(2)}) collective-permute-start(bf16[512,256]{1,0:T(8,128)(2,1)S(1)} %copy-done.9), channel_id=1, source_target_pairs={{0,0},{1,128},{2,256},{3,384},{4,4},{5,132},{6,260},{7,388},{8,8},... | collective-permute-start | bytes 786440 | tf_op jit(solution)/shard_map/ppermute | solution.py:207
  25.4 9.8 %collective-permute-done.1 = bf16[512,256]{1,0:T(8,128)(2,1)S(1)} collective-permute-done((bf16[512,256]{1,0:T(8,128)(2,1)S(1)}, bf16[512,256]{1,0:T(8,128)(2,1)S(1)}, u32[]{:S(2)}, u32[]{:S(2)}) %collective-permute-start.1) | collective-permute-done | bytes 262176 | tf_op jit(solution)/shard_map/ppermute | solution.py:207
  35.2 0.0 collective-permute-done.oth_ref
  35.2 0.3 all-to-all-done.q_ref
  35.5 0.4 copy-done.4
  35.9 0.0 all-gather.2.cloned.1.call-update
  36.0 0.0 copy-done.7
  36.0 0.1 select_convert_fusion.hide_ref
  36.1 0.0 copy-start.2
  36.1 7.4 %shard_map.91 = bf16[16,32,640]{2,1,0:T(8,128)(2,1)} custom-call(bf16[16,32,512]{2,1,0:T(8,128)(2,1)S(1)} %all-to-all-done.q_ref, bf16[512,128]{1,0:T(8,128)(2,1)S(1)} %select_convert_fusion.hide_ref, bf16[2064,128]{1,0:T(8,128)(2,1)S(1)} %fusion.1.own_ref, bf16[2064,128]{1,0:T(8,128)(2,1)S(1)} %collective-permute-done.oth_ref), custom_call_target="tpu_custom_call" | custom-call | flops 2147483648 | bytes 2097152 | tf_op jit(solution)/shard_map/pallas_call | solution.py:166
  43.5 12.9 %all-to-all-start.1 = ((bf16[16,32,640]{2,1,0:T(8,128)(2,1)}), bf16[16,32,640]{2,1,0:T(8,128)(2,1)S(1)}, u32[]{:S(2)}, u32[]{:S(2)}) async-start(bf16[16,32,640]{2,1,0:T(8,128)(2,1)} %shard_map.91), calls=%async_computation.1 | async-start | bytes 1310720 | tf_op jit(solution)/shard_map/all_to_all | solution.py:245
  56.4 0.0 copy-done.8
  56.4 0.1 copy.10.len_ref
  56.5 0.0 copy-done.2
  56.5 1.1 shard_map.92
  57.6 13.0 %all-to-all-done.1.got_ref = bf16[16,32,640]{2,1,0:T(8,128)(2,1)S(1)} async-done(((bf16[16,32,640]{2,1,0:T(8,128)(2,1)}), bf16[16,32,640]{2,1,0:T(8,128)(2,1)S(1)}, u32[]{:S(2)}, u32[]{:S(2)}) %all-to-all-start.1) | async-done | bytes 655392 | tf_op jit(solution)/shard_map/all_to_all | solution.py:245
  70.6 0.7 shard_map.93
  71.4 1.9 %collective-permute-start.2 = (bf16[32,512]{1,0:T(8,128)(2,1)S(1)}, bf16[32,512]{1,0:T(8,128)(2,1)S(1)}, u32[]{:S(2)}, u32[]{:S(2)}) collective-permute-start(bf16[32,512]{1,0:T(8,128)(2,1)S(1)} %shard_map.93), channel_id=1, source_target_pairs={{0,0},{1,128},{2,256},{3,384},{4,16},{5,144},{6,272},{7,400},{8,32... | collective-permute-start | bytes 98312 | tf_op jit(solution)/shard_map/ppermute | solution.py:258
  73.3 9.0 %collective-permute-done.2 = bf16[32,512]{1,0:T(8,128)(2,1)S(1)} collective-permute-done((bf16[32,512]{1,0:T(8,128)(2,1)S(1)}, bf16[32,512]{1,0:T(8,128)(2,1)S(1)}, u32[]{:S(2)}, u32[]{:S(2)}) %collective-permute-start.2) | collective-permute-done | bytes 32800 | tf_op jit(solution)/shard_map/ppermute | solution.py:258
  82.4 16.7 %all_to_all.20.att_ref = bf16[8,32,512]{2,1,0:T(8,128)(2,1)S(1)} all-to-all(bf16[8,32,512]{2,1,0:T(8,128)(2,1)S(1)} %broadcast_in_dim.30), channel_id=1, replica_groups={{0,16,32,48,64,80,96,112},{128,144,160,176,192,208,224,240},{256,272,28..., dimensions={0} | all-to-all | bytes 524288 | tf_op jit(solution)/shard_map/all_to_all | solution.py:259
  99.1 2.2 %copy-done = bf16[8192,256]{1,0:T(8,128)(2,1)S(1)} copy-done((bf16[8192,256]{1,0:T(8,128)(2,1)S(1)}, bf16[8192,256]{1,0:T(8,128)(2,1)}, u32[]{:S(2)}) %copy-start) | copy-done | bytes 4194328
  101.3 0.8 shard_map.94
  102.1 14.0 %all_to_all.21.part_ref = bf16[4,64,256]{2,1,0:T(8,128)(2,1)S(1)} all-to-all(bf16[4,64,256]{2,1,0:T(8,128)(2,1)S(1)} %shard_map.94), channel_id=1, replica_groups={{0,128,256,384},{16,144,272,400},{32,160,288,416},{48,176,304,432},{64,..., dimensions={0} | all-to-all | bytes 262144 | tf_op jit(solution)/shard_map/all_to_all | solution.py:275
  116.1 0.6 shard_map.95
  (18 shorter events, 0.1 us)
Async XLA Ops:
  6.5 11.3 %copy-start.10 = (s32[8]{0:T(128)S(1)}, s32[8]{0:T(128)}, u32[]{:S(2)}) copy-start(s32[8]{0:T(128)} %param.13) | copy-start | bytes 100
  6.5 11.3 %copy-start.6 = (bf16[1,1024,128]{2,1,0:T(8,128)(2,1)S(1)}, bf16[1,1024,128]{2,1,0:T(8,128)(2,1)}, u32[]{:S(2)}) copy-start(bf16[1,1024,128]{2,1,0:T(8,128)(2,1)} %param.15) | copy-start | bytes 786436
  6.5 11.3 %copy-start.5 = (bf16[1,1024,128]{2,1,0:T(8,128)(2,1)S(1)}, bf16[1,1024,128]{2,1,0:T(8,128)(2,1)}, u32[]{:S(2)}) copy-start(bf16[1,1024,128]{2,1,0:T(8,128)(2,1)} %param.16) | copy-start | bytes 786436
  8.2 11.8 %copy-start.9 = (bf16[512,256]{1,0:T(8,128)(2,1)S(1)}, bf16[512,256]{1,0:T(8,128)(2,1)}, u32[]{:S(2)}) copy-start(bf16[512,256]{1,0:T(8,128)(2,1)} %param.19) | copy-start | bytes 786436
  8.2 27.7 %copy-start.7 = (s32[1024]{0:T(1024)S(1)}, s32[1024]{0:T(1024)}, u32[]{:S(2)}) copy-start(s32[1024]{0:T(1024)} %param.12) | copy-start | bytes 12292
  8.2 27.3 %all-to-all-start = ((bf16[16,32,512]{2,1,0:T(8,128)(2,1)}), bf16[16,32,512]{2,1,0:T(8,128)(2,1)S(1)}, u32[]{:S(2)}, u32[]{:S(2)}) async-start(bf16[16,32,512]{2,1,0:T(8,128)(2,1)} %broadcast_in_dim.14), calls=%async_computation | async-start | bytes 1048576 | tf_op jit(solution)/shard_map/all_to_all | solution.py:199
  17.8 81.3 %all-gather.2.cloned.1.call-start = ((), (), s32[]{:S(2)}) async-start(), calls=%async_computation.4 | async-start | bytes 4456448 | tf_op jit(solution)/shard_map/all_gather | solution.py:244
  17.9 17.3 %collective-permute-start = (bf16[2064,128]{1,0:T(8,128)(2,1)S(1)}, bf16[2064,128]{1,0:T(8,128)(2,1)S(1)}, u32[]{:S(2)}, u32[]{:S(2)}) collective-permute-start(bf16[2064,128]{1,0:T(8,128)(2,1)S(1)} %fusion.1.own_ref), channel_id=1, source_target_pairs={{0,128},{16,144},{32,160},{48,176},{64,192},{80,208},{96,224},{112... | collective-permute-start | bytes 1585160 | tf_op jit(solution)/shard_map/ppermute | solution.py:197
  20.0 15.1 %collective-permute-start.1 = (bf16[512,256]{1,0:T(8,128)(2,1)S(1)}, bf16[512,256]{1,0:T(8,128)(2,1)S(1)}, u32[]{:S(2)}, u32[]{:S(2)}) collective-permute-start(bf16[512,256]{1,0:T(8,128)(2,1)S(1)} %copy-done.9), channel_id=1, source_target_pairs={{0,0},{1,128},{2,256},{3,384},{4,4},{5,132},{6,260},{7,388},{8,8},... | collective-permute-start | bytes 786440 | tf_op jit(solution)/shard_map/ppermute | solution.py:207
  35.2 0.7 copy-start.4
  36.1 20.4 %copy-start.2 = (bf16[1,32,128,128]{3,2,1,0:T(8,128)(2,1)S(1)}, bf16[1,32,128,128]{3,2,1,0:T(8,128)(2,1)}, u32[]{:S(2)}) copy-start(bf16[1,32,128,128]{3,2,1,0:T(8,128)(2,1)} %param.18) | copy-start | bytes 3145732
  43.5 12.9 %copy-start.8 = (s32[32]{0:T(128)S(1)}, s32[32]{0:T(128)}, u32[]{:S(2)}) copy-start(s32[32]{0:T(128)} %param.14) | copy-start | bytes 388
  43.5 13.0 %copy-start.1 = (bf16[1,32,128,128]{3,2,1,0:T(8,128)(2,1)S(1)}, bf16[1,32,128,128]{3,2,1,0:T(8,128)(2,1)}, u32[]{:S(2)}) copy-start(bf16[1,32,128,128]{3,2,1,0:T(8,128)(2,1)} %param.17) | copy-start | bytes 3145732
  43.5 13.0 %copy-start.3 = (bf16[32,512]{1,0:T(8,128)(2,1)S(1)}, bf16[32,512]{1,0:T(8,128)(2,1)}, u32[]{:S(2)}) copy-start(bf16[32,512]{1,0:T(8,128)(2,1)} %q_ref.1) | copy-start | bytes 98308
  43.5 27.1 %all-to-all-start.1 = ((bf16[16,32,640]{2,1,0:T(8,128)(2,1)}), bf16[16,32,640]{2,1,0:T(8,128)(2,1)S(1)}, u32[]{:S(2)}, u32[]{:S(2)}) async-start(bf16[16,32,640]{2,1,0:T(8,128)(2,1)} %shard_map.91), calls=%async_computation.1 | async-start | bytes 1310720 | tf_op jit(solution)/shard_map/all_to_all | solution.py:245
  71.4 11.0 %collective-permute-start.2 = (bf16[32,512]{1,0:T(8,128)(2,1)S(1)}, bf16[32,512]{1,0:T(8,128)(2,1)S(1)}, u32[]{:S(2)}, u32[]{:S(2)}) collective-permute-start(bf16[32,512]{1,0:T(8,128)(2,1)S(1)} %shard_map.93), channel_id=1, source_target_pairs={{0,0},{1,128},{2,256},{3,384},{4,16},{5,144},{6,272},{7,400},{8,32... | collective-permute-start | bytes 98312 | tf_op jit(solution)/shard_map/ppermute | solution.py:258
  99.1 2.2 %copy-start = (bf16[8192,256]{1,0:T(8,128)(2,1)S(1)}, bf16[8192,256]{1,0:T(8,128)(2,1)}, u32[]{:S(2)}) copy-start(bf16[8192,256]{1,0:T(8,128)(2,1)} %all-gather.2.cloned.1.call-done.w_ref) | copy-start | bytes 12582916
Sparse Core Ops, SparseCore 0:
  36.1 51.8 all-gather.1

commit v3 on v2

--- a/solution.py
+++ b/solution.py
@@ -14,6 +14,7 @@
 ROWS = 32
 MEMBERS = 16
 LANES = 128
+STATS = 16
 TAB = 16
 HIDE = -1e30
 FLOOR = -262144.0
@@ -75,23 +76,34 @@
         part = slice(j * ROWS, (j + 1) * ROWS)
         stat = jnp.where(lane == j, high[part] * SCALE, stat)
         stat = jnp.where(lane == HEADS + j, totals[part], stat)
-    stat_ref[...] = stat
-
-
-def owner_kernel(q_ref, hide_ref, own_ref, oth_ref, out_ref, keys_ref):
+    stat = jnp.concatenate([stat, jnp.zeros((LANES - ROWS, LANES), f32)], axis=0)
+    stat_ref[...] = stat.T[: 2 * HEADS]
+
+
+def keys_kernel(own_ref, oth_ref, keys_ref, values_ref):
     tokens = (own_ref.shape[0] - TAB) // 2
     slots = tokens // LANES
     lane = lax.broadcasted_iota(jnp.int32, (LANES, LANES), 1)
     for o, ref in enumerate((own_ref, oth_ref)):
         table = ref[2 * tokens : 2 * tokens + TAB, :].astype(f32)
         keys_ref[o, :, :HD] = ref[:tokens, :]
+        values_ref[o] = ref[tokens : 2 * tokens, :]
         for s in range(slots):
             other = (lane < CPP) & (lane.astype(f32) != table[0:1, s : s + 1])
             keys_ref[o, s * LANES : (s + 1) * LANES, HD:] = jnp.where(other, 1.0, 0.0).astype(bf16)
+
+
+def owner_kernel(q_ref, hide_ref, keys_ref, values_ref, out_ref):
     branches = MEMBERS * ROWS
     block = 512
     lane = lax.broadcasted_iota(jnp.int32, (block, LANES), 1)
     per = block // ROWS
+    unit = jnp.where(
+        lax.broadcasted_iota(jnp.int32, (STATS, LANES), 0)
+        == lax.broadcasted_iota(jnp.int32, (STATS, LANES), 1),
+        1.0,
+        0.0,
+    ).astype(bf16)
     for r in range(branches // block):
         hide = hide_ref[r * block : (r + 1) * block, :]
         stat = jnp.zeros((block, LANES), f32)
@@ -99,12 +111,12 @@
             q = q_ref[r * per : (r + 1) * per, :, j * HD : (j + 1) * HD].reshape(block, HD)
             q = jnp.concatenate([q, hide], axis=1)
             parts = []
-            for o, ref in enumerate((own_ref, oth_ref)):
+            for o in range(keys_ref.shape[0]):
                 scores = nt_dot(q, keys_ref[o])
                 high = jnp.maximum(jnp.max(scores, axis=1, keepdims=True), FLOOR)
                 weights = jnp.exp2((scores - high) * SCALE)
                 totals = jnp.sum(weights, axis=1, keepdims=True)
-                numer = jnp.dot(weights.astype(bf16), ref[tokens : 2 * tokens, :], preferred_element_type=f32)
+                numer = jnp.dot(weights.astype(bf16), values_ref[o], preferred_element_type=f32)
                 parts.append((high * SCALE, totals, numer))
             (ha, ta, na), (hb, tb, nb) = parts
             high = jnp.maximum(ha, hb).astype(bf16).astype(f32)
@@ -112,35 +124,38 @@
             numer = na * fa + nb * fb
             totals = ta * fa + tb * fb
             coarse = totals.astype(bf16).astype(f32)
-            out_ref[r * per : (r + 1) * per, :, j * HD : (j + 1) * HD] = numer.astype(bf16).reshape(per, ROWS, HD)
+            out_ref[r * per : (r + 1) * per, j * ROWS : (j + 1) * ROWS, :] = numer.astype(bf16).reshape(per, ROWS, HD)
             stat = jnp.where(lane == j, high, stat)
             stat = jnp.where(lane == HEADS + j, coarse, stat)
             stat = jnp.where(lane == 2 * HEADS + j, totals - coarse, stat)
-        out_ref[r * per : (r + 1) * per, :, HEADS * HD :] = stat.astype(bf16).reshape(per, ROWS, LANES)
+        stat = stat.astype(bf16)
+        for i in range(per):
+            turned = nt_dot(unit, stat[i * ROWS : (i + 1) * ROWS])
+            out_ref[r * per + i, HEADS * ROWS :, :ROWS] = turned.astype(bf16)
 
 
 def join_kernel(got_ref, numer_ref, stat_ref, out_ref):
-    wide = HEADS * HD
     own = stat_ref[...]
-    top = own
-    for i in range(MEMBERS):
-        top = jnp.maximum(top, got_ref[i, :, wide:].astype(f32))
-    lane = lax.broadcasted_iota(jnp.int32, (ROWS, LANES), 1)
-    shift = lane < HEADS
-    top = jnp.where(shift, top, 0.0)
-    fac_own = jnp.exp2(jnp.where(shift, own, 0.0) - top)
-    numer = [numer_ref[:, j * HD : (j + 1) * HD] * fac_own[:, j : j + 1] for j in range(HEADS)]
-    total = [own[:, HEADS + j : HEADS + j + 1] * fac_own[:, j : j + 1] for j in range(HEADS)]
-    for i in range(MEMBERS):
-        stat = got_ref[i, :, wide:].astype(f32)
-        fac = jnp.exp2(jnp.where(shift, stat, 0.0) - top)
-        for j in range(HEADS):
-            f = fac[:, j : j + 1]
-            numer[j] = numer[j] + got_ref[i, :, j * HD : (j + 1) * HD].astype(f32) * f
-            t = stat[:, HEADS + j : HEADS + j + 1] + stat[:, 2 * HEADS + j : 2 * HEADS + j + 1]
-            total[j] = total[j] + t * f
+    wide = HEADS * ROWS
+    stats = [got_ref[i, wide:, :].astype(f32) for i in range(MEMBERS)]
+    top = own[:HEADS]
+    for stat in stats:
+        top = jnp.maximum(top, stat[:HEADS])
+    factors = [jnp.exp2(own[:HEADS] - top)]
+    total = own[HEADS:] * factors[0]
+    for stat in stats:
+        factors.append(jnp.exp2(stat[:HEADS] - top))
+        total = total + (stat[HEADS : 2 * HEADS] + stat[2 * HEADS : 3 * HEADS]) * factors[-1]
+    inverse = 1.0 / total
+    rows = jnp.concatenate([f * inverse for f in factors], axis=0)
+    rows = jnp.concatenate([rows, jnp.zeros((LANES - rows.shape[0], LANES), f32)], axis=0)
+    columns = rows.T[:ROWS]
     for j in range(HEADS):
-        out_ref[:, j * HD : (j + 1) * HD] = (numer[j] / total[j]).astype(bf16)
+        acc = numer_ref[:, j * HD : (j + 1) * HD] * columns[:, j : j + 1]
+        for i in range(MEMBERS):
+            at = (i + 1) * HEADS + j
+            acc = acc + got_ref[i, j * ROWS : (j + 1) * ROWS, :].astype(f32) * columns[:, at : at + 1]
+        out_ref[:, j * HD : (j + 1) * HD] = acc.astype(bf16)
 
 
 def project_kernel(att_ref, w_ref, out_ref):
@@ -162,11 +177,10 @@
     out_ref[...] = acc.astype(bf16)
 
 
-def call(kernel, out_shape, *args, flops=0, moved=0, scratch=()):
+def call(kernel, out_shape, *args, flops=0, moved=0):
     return pl.pallas_call(
         kernel,
         out_shape=out_shape,
-        scratch_shapes=scratch,
         compiler_params=pltpu.CompilerParams(vmem_limit_bytes=40 * 2**20),
         cost_estimate=pl.CostEstimate(flops=flops, bytes_accessed=moved, transcendentals=0),
     )(*args)
@@ -205,7 +219,19 @@
         axis_index_groups=GROUPS,
     )
     weight = lax.ppermute(out_weight, ("pool", "head"), WEIGHT_MOVES)
-    got, oth, weight = lax.optimization_barrier((got, oth, weight))
+    keys, values = call(
+        keys_kernel,
+        (
+            jax.ShapeDtypeStruct((2, prefix_keys.shape[1], 2 * HD), bf16),
+            jax.ShapeDtypeStruct((2, prefix_keys.shape[1], HD), bf16),
+        ),
+        own,
+        oth,
+        flops=20 * 2**30,
+        moved=2 * 2**20,
+    )
+    got, weight, keys, values = lax.optimization_barrier((got, weight, keys, values))
+    weight = lax.all_gather(weight, "head", axis=0, tiled=True)
 
     span = NY * ROWS
     outer = (x == GROUP_X[0][0]) | (x == GROUP_X[0][1])
@@ -220,7 +246,7 @@
         suffix_kernel,
         (
             jax.ShapeDtypeStruct((ROWS, HEADS * HD), f32),
-            jax.ShapeDtypeStruct((ROWS, LANES), f32),
+            jax.ShapeDtypeStruct((2 * HEADS, LANES), f32),
         ),
         queries,
         suffix_len[:, None],
@@ -232,16 +258,14 @@
 
     state = call(
         owner_kernel,
-        jax.ShapeDtypeStruct((MEMBERS, ROWS, HEADS * HD + LANES), bf16),
+        jax.ShapeDtypeStruct((MEMBERS, HEADS * ROWS + STATS, HD), bf16),
         got,
         hide,
-        own,
-        oth,
+        keys,
+        values,
         flops=4 * 2048 * 2048 * 128,
         moved=2 * 2**20,
-        scratch=[pltpu.VMEM((2, prefix_keys.shape[1], 2 * HD), bf16)],
-    )
-    weight = lax.all_gather(weight, "head", axis=0, tiled=True)
+    )
     state = lax.all_to_all(
         state, "pool", split_axis=0, concat_axis=0, tiled=True, axis_index_groups=GROUPS
     )

time: 124 us -> 122 us (0.984)
  the two profiles are of different devices: /device:TPU:64 before, /device:TPU:384 now
where the time goes in v3:
time: 122 us
  waiting for transfers between devices  37.9 us (31%)
  blocking collectives  28.8 us (24%)
  starting transfers between devices  23.7 us (19%)
  between operations  13.6 us (11%)
  Pallas kernels  10.6 us (9%)
  local copies, waits for them, and re-layouts  5.37 us (4%)
  other arithmetic  1.88 us (2%)
    all_to_all x1, blocking collectives, on_device(): lax.all_to_all(jnp.broadcast_to(attention[None], (NY,) + attention.shape)...  20.4 us
    all_to_all x1, waiting for transfers between devices, on_device(): lax.all_to_all(state, 'pool', split_axis=0, concat_axis=0, tiled=True, ax...  15.6 us
    all_to_all x1, waiting for transfers between devices, on_device(): lax.all_to_all(jnp.broadcast_to(queries[None], (MEMBERS,) + queries.shape...  12.4 us
    pallas_call x6, Pallas kernels, call(): pl.pallas_call(kernel, out_shape=out_shape, compiler_params=pltpu.Compile...  10.6 us
    ppermute x1, waiting for transfers between devices, on_device(): attention = lax.ppermute(attention, ('pool', 'head'), ATTENTION_MOVES)  8.85 us
    all_to_all x1, starting transfers between devices, on_device(): lax.all_to_all(jnp.broadcast_to(queries[None], (MEMBERS,) + queries.shape...  8.74 us
    all_to_all x1, blocking collectives, on_device(): lax.all_to_all(partial, 'pool', split_axis=0, concat_axis=0, tiled=True,...  8.36 us
    all_to_all x1, starting transfers between devices, on_device(): lax.all_to_all(state, 'pool', split_axis=0, concat_axis=0, tiled=True, ax...  8.03 us
  transfers between devices with their start and end apart: 6, of which 4 were waited for; matrix products, arithmetic and copies ran while one was open for 1% of the time, Pallas kernels for 8%

profile of v3, /device:TPU:384, one launch (start us, length us, event | category | flops | bytes accessed | tf_op | source)
XLA Modules:
  0.0 121.9 jit_solution(3804083590108258968)
XLA Ops:
  6.5 0.7 convert_bitcast_fusion
  7.2 1.1 fusion.1.own_ref
  8.3 3.4 %collective-permute-start.1 = (bf16[2064,128]{1,0:T(8,128)(2,1)S(1)}, bf16[2064,128]{1,0:T(8,128)(2,1)S(1)}, u32[]{:S(2)}, u32[]{:S(2)}) collective-permute-start(bf16[2064,128]{1,0:T(8,128)(2,1)S(1)} %fusion.1.own_ref), channel_id=1, source_target_pairs={{0,128},{16,144},{32,160},{48,176},{64,192},{80,208},{96,224},{112... | collective-permute-start | bytes 1585160 | tf_op jit(solution)/shard_map/ppermute | solution.py:211
  11.7 0.0 copy-done.3
  11.7 0.9 broadcast_in_dim.14
  12.6 8.7 %all-to-all-start = ((bf16[16,32,512]{2,1,0:T(8,128)(2,1)}), bf16[16,32,512]{2,1,0:T(8,128)(2,1)S(1)}, u32[]{:S(2)}, u32[]{:S(2)}) async-start(bf16[16,32,512]{2,1,0:T(8,128)(2,1)} %broadcast_in_dim.14), calls=%async_computation | async-start | bytes 1048576 | tf_op jit(solution)/shard_map/all_to_all | solution.py:213
  21.3 0.0 copy-start.7
  21.3 0.0 all-gather.2.cloned.1.call-start
  21.4 1.6 %collective-permute-start = (bf16[512,256]{1,0:T(8,128)(2,1)}, bf16[512,256]{1,0:T(8,128)(2,1)S(1)}, u32[]{:S(2)}, u32[]{:S(2)}) collective-permute-start(bf16[512,256]{1,0:T(8,128)(2,1)} %param.19), channel_id=1, source_target_pairs={{0,0},{1,128},{2,256},{3,384},{4,4},{5,132},{6,260},{7,388},{8,8},... | collective-permute-start | bytes 786440 | tf_op jit(solution)/shard_map/ppermute | solution.py:221
  23.0 1.0 collective-permute-done.1.oth_ref
  23.9 0.2 shard_map.91
  24.2 0.0 copy-start.4
  24.2 1.0 copy-done.4
  25.1 0.0 collective-permute-done
  25.2 12.4 %all-to-all-done.q_ref = bf16[16,32,512]{2,1,0:T(8,128)(2,1)S(1)} async-done(((bf16[16,32,512]{2,1,0:T(8,128)(2,1)}), bf16[16,32,512]{2,1,0:T(8,128)(2,1)S(1)}, u32[]{:S(2)}, u32[]{:S(2)}) %all-to-all-start) | async-done | bytes 524320 | tf_op jit(solution)/shard_map/all_to_all | solution.py:213
  37.6 0.0 copy-done.6
  37.6 0.0 all-gather.2.cloned.1.call-update
  37.7 0.1 select_convert_fusion.hide_ref
  37.8 1.2 copy-done.5
  39.1 7.2 %shard_map.92 = bf16[16,144,128]{2,1,0:T(8,128)(2,1)} custom-call(bf16[16,32,512]{2,1,0:T(8,128)(2,1)S(1)} %all-to-all-done.q_ref, bf16[512,128]{1,0:T(8,128)(2,1)S(1)} %select_convert_fusion.hide_ref, bf16[2,1024,256]{2,1,0:T(8,128)(2,1)S(1)} %copy-done.5, bf16[2,1024,128]{2,1,0:T(8,128)(2,1)S(1)} %get-tuple-element.29.values_ref), custom_call_target="tpu_custom_call" | custom-call | flops 2147483648 | bytes 2097152 | tf_op jit(solution)/shard_map/pallas_call | solution.py:181
  46.2 8.0 %all-to-all-start.1 = ((bf16[16,144,128]{2,1,0:T(8,128)(2,1)}), bf16[16,144,128]{2,1,0:T(8,128)(2,1)S(1)}, u32[]{:S(2)}, u32[]{:S(2)}) async-start(bf16[16,144,128]{2,1,0:T(8,128)(2,1)} %shard_map.92), calls=%async_computation.1 | async-start | bytes 1179648 | tf_op jit(solution)/shard_map/all_to_all | solution.py:269
  54.3 0.1 copy.10.len_ref
  54.4 1.1 shard_map.93
  55.5 15.6 %all-to-all-done.1.got_ref = bf16[16,144,128]{2,1,0:T(8,128)(2,1)S(1)} async-done(((bf16[16,144,128]{2,1,0:T(8,128)(2,1)}), bf16[16,144,128]{2,1,0:T(8,128)(2,1)S(1)}, u32[]{:S(2)}, u32[]{:S(2)}) %all-to-all-start.1) | async-done | bytes 589856 | tf_op jit(solution)/shard_map/all_to_all | solution.py:269
  71.1 0.6 shard_map.94
  71.8 1.9 %collective-permute-start.2 = (bf16[32,512]{1,0:T(8,128)(2,1)S(1)}, bf16[32,512]{1,0:T(8,128)(2,1)S(1)}, u32[]{:S(2)}, u32[]{:S(2)}) collective-permute-start(bf16[32,512]{1,0:T(8,128)(2,1)S(1)} %shard_map.94), channel_id=1, source_target_pairs={{0,0},{1,128},{2,256},{3,384},{4,16},{5,144},{6,272},{7,400},{8,32... | collective-permute-start | bytes 98312 | tf_op jit(solution)/shard_map/ppermute | solution.py:282
  73.7 8.9 %collective-permute-done.2 = bf16[32,512]{1,0:T(8,128)(2,1)S(1)} collective-permute-done((bf16[32,512]{1,0:T(8,128)(2,1)S(1)}, bf16[32,512]{1,0:T(8,128)(2,1)S(1)}, u32[]{:S(2)}, u32[]{:S(2)}) %collective-permute-start.2) | collective-permute-done | bytes 32800 | tf_op jit(solution)/shard_map/ppermute | solution.py:282
  82.6 20.4 %all_to_all.20.att_ref = bf16[8,32,512]{2,1,0:T(8,128)(2,1)S(1)} all-to-all(bf16[8,32,512]{2,1,0:T(8,128)(2,1)S(1)} %broadcast_in_dim.30), channel_id=1, replica_groups={{0,16,32,48,64,80,96,112},{128,144,160,176,192,208,224,240},{256,272,28..., dimensions={0} | all-to-all | bytes 524288 | tf_op jit(solution)/shard_map/all_to_all | solution.py:283
  103.0 2.2 %copy-done = bf16[8192,256]{1,0:T(8,128)(2,1)S(1)} copy-done((bf16[8192,256]{1,0:T(8,128)(2,1)S(1)}, bf16[8192,256]{1,0:T(8,128)(2,1)}, u32[]{:S(2)}) %copy-start) | copy-done | bytes 4194328
  105.2 0.8 shard_map.95
  106.0 8.4 %all_to_all.21.part_ref = bf16[4,64,256]{2,1,0:T(8,128)(2,1)S(1)} all-to-all(bf16[4,64,256]{2,1,0:T(8,128)(2,1)S(1)} %shard_map.95), channel_id=1, replica_groups={{0,128,256,384},{16,144,272,400},{32,160,288,416},{48,176,304,432},{64,..., dimensions={0} | all-to-all | bytes 262144 | tf_op jit(solution)/shard_map/all_to_all | solution.py:299
  114.4 0.6 shard_map.96
  (15 shorter events, 0.1 us)
Async XLA Ops:
  6.5 5.2 %copy-start.3 = (bf16[32,512]{1,0:T(8,128)(2,1)S(1)}, bf16[32,512]{1,0:T(8,128)(2,1)}, u32[]{:S(2)}) copy-start(bf16[32,512]{1,0:T(8,128)(2,1)} %q_ref.1) | copy-start | bytes 98308
  8.3 15.6 %collective-permute-start.1 = (bf16[2064,128]{1,0:T(8,128)(2,1)S(1)}, bf16[2064,128]{1,0:T(8,128)(2,1)S(1)}, u32[]{:S(2)}, u32[]{:S(2)}) collective-permute-start(bf16[2064,128]{1,0:T(8,128)(2,1)S(1)} %fusion.1.own_ref), channel_id=1, source_target_pairs={{0,128},{16,144},{32,160},{48,176},{64,192},{80,208},{96,224},{112... | collective-permute-start | bytes 1585160 | tf_op jit(solution)/shard_map/ppermute | solution.py:211
  12.6 25.1 %all-to-all-start = ((bf16[16,32,512]{2,1,0:T(8,128)(2,1)}), bf16[16,32,512]{2,1,0:T(8,128)(2,1)S(1)}, u32[]{:S(2)}, u32[]{:S(2)}) async-start(bf16[16,32,512]{2,1,0:T(8,128)(2,1)} %broadcast_in_dim.14), calls=%async_computation | async-start | bytes 1048576 | tf_op jit(solution)/shard_map/all_to_all | solution.py:213
  21.3 16.4 %copy-start.7 = (s32[1024]{0:T(1024)S(1)}, s32[1024]{0:T(1024)}, u32[]{:S(2)}) copy-start(s32[1024]{0:T(1024)} %param.12) | copy-start | bytes 12292
  21.3 81.7 %all-gather.2.cloned.1.call-start = ((), (), s32[]{:S(2)}) async-start(), calls=%async_computation.4 | async-start | bytes 4456448 | tf_op jit(solution)/shard_map/all_gather | solution.py:234
  21.4 3.8 %collective-permute-start = (bf16[512,256]{1,0:T(8,128)(2,1)}, bf16[512,256]{1,0:T(8,128)(2,1)S(1)}, u32[]{:S(2)}, u32[]{:S(2)}) collective-permute-start(bf16[512,256]{1,0:T(8,128)(2,1)} %param.19), channel_id=1, source_target_pairs={{0,0},{1,128},{2,256},{3,384},{4,4},{5,132},{6,260},{7,388},{8,8},... | collective-permute-start | bytes 786440 | tf_op jit(solution)/shard_map/ppermute | solution.py:221
  24.2 1.0 copy-start.4
  25.1 12.5 %copy-start.6 = (bf16[512,256]{1,0:T(8,128)(2,1)}, bf16[512,256]{1,0:T(8,128)(2,1)S(1)}, u32[]{:S(2)}) copy-start(bf16[512,256]{1,0:T(8,128)(2,1)S(1)} %collective-permute-done) | copy-start | bytes 786436
  37.8 1.2 %copy-start.5 = (bf16[2,1024,256]{2,1,0:T(8,128)(2,1)S(1)}, bf16[2,1024,256]{2,1,0:T(8,128)(2,1)}, u32[]{:S(2)}) copy-start(bf16[2,1024,256]{2,1,0:T(8,128)(2,1)} %copy-done.4) | copy-start | bytes 3145732
  39.1 15.3 %copy-start.2 = (bf16[1,32,128,128]{3,2,1,0:T(8,128)(2,1)S(1)}, bf16[1,32,128,128]{3,2,1,0:T(8,128)(2,1)}, u32[]{:S(2)}) copy-start(bf16[1,32,128,128]{3,2,1,0:T(8,128)(2,1)} %param.18) | copy-start | bytes 3145732
  46.2 8.0 %copy-start.8 = (s32[32]{0:T(128)S(1)}, s32[32]{0:T(128)}, u32[]{:S(2)}) copy-start(s32[32]{0:T(128)} %param.14) | copy-start | bytes 388
  46.2 8.1 %copy-start.1 = (bf16[1,32,128,128]{3,2,1,0:T(8,128)(2,1)S(1)}, bf16[1,32,128,128]{3,2,1,0:T(8,128)(2,1)}, u32[]{:S(2)}) copy-start(bf16[1,32,128,128]{3,2,1,0:T(8,128)(2,1)} %param.17) | copy-start | bytes 3145732
  46.2 24.9 %all-to-all-start.1 = ((bf16[16,144,128]{2,1,0:T(8,128)(2,1)}), bf16[16,144,128]{2,1,0:T(8,128)(2,1)S(1)}, u32[]{:S(2)}, u32[]{:S(2)}) async-start(bf16[16,144,128]{2,1,0:T(8,128)(2,1)} %shard_map.92), calls=%async_computation.1 | async-start | bytes 1179648 | tf_op jit(solution)/shard_map/all_to_all | solution.py:269
  71.8 10.8 %collective-permute-start.2 = (bf16[32,512]{1,0:T(8,128)(2,1)S(1)}, bf16[32,512]{1,0:T(8,128)(2,1)S(1)}, u32[]{:S(2)}, u32[]{:S(2)}) collective-permute-start(bf16[32,512]{1,0:T(8,128)(2,1)S(1)} %shard_map.94), channel_id=1, source_target_pairs={{0,0},{1,128},{2,256},{3,384},{4,16},{5,144},{6,272},{7,400},{8,32... | collective-permute-start | bytes 98312 | tf_op jit(solution)/shard_map/ppermute | solution.py:282
  103.0 2.2 %copy-start = (bf16[8192,256]{1,0:T(8,128)(2,1)S(1)}, bf16[8192,256]{1,0:T(8,128)(2,1)}, u32[]{:S(2)}) copy-start(bf16[8192,256]{1,0:T(8,128)(2,1)} %all-gather.2.cloned.1.call-done.w_ref) | copy-start | bytes 12582916
Sparse Core Ops, SparseCore 0:
  37.8 41.9 all-gather.1

commit v4 on v3

--- a/solution.py
+++ b/solution.py
@@ -37,7 +37,11 @@
 EVERY = [(x, y, h) for x in range(NX) for y in range(NY) for h in range(NH)]
 WEIGHT_MOVES = [(place(x, y, h), place(h % NX, y, h - h % NX + x)) for x, y, h in EVERY]
 ATTENTION_MOVES = [
-    (place(x, y, h), place(h % NX, (y % 2) * NX + h // NX, NX * x + y // 2)) for x, y, h in EVERY
+    (
+        place(x, y, h),
+        place(h % NX, (y + h // NX if y % 2 else y - h // NX) % NY, NX * x + y // 2),
+    )
+    for x, y, h in EVERY
 ]
 
 
@@ -158,13 +162,15 @@
         out_ref[:, j * HD : (j + 1) * HD] = acc.astype(bf16)
 
 
-def project_kernel(att_ref, w_ref, out_ref):
+def project_kernel(first_ref, att_ref, w_ref, out_ref):
     depth = att_ref.shape[2]
     half = att_ref.shape[0] // 2
+    first = first_ref[0]
     for c in range(out_ref.shape[0]):
         acc = jnp.zeros(out_ref.shape[1:], f32)
         for k in range(half):
-            rows = jnp.concatenate([att_ref[k], att_ref[half + k]], axis=0)
+            down, up = (first + NY - k) % NY, (first + 1 + k) % NY
+            rows = jnp.concatenate([att_ref[down], att_ref[up]], axis=0)
             i = k * out_ref.shape[0] + c
             acc = acc + jnp.dot(rows, w_ref[i * depth : (i + 1) * depth, :], preferred_element_type=f32)
         out_ref[c] = acc.astype(out_ref.dtype)
@@ -231,7 +237,6 @@
         moved=2 * 2**20,
     )
     got, weight, keys, values = lax.optimization_barrier((got, weight, keys, values))
-    weight = lax.all_gather(weight, "head", axis=0, tiled=True)
 
     span = NY * ROWS
     outer = (x == GROUP_X[0][0]) | (x == GROUP_X[0][1])
@@ -266,6 +271,8 @@
         flops=4 * 2048 * 2048 * 128,
         moved=2 * 2**20,
     )
+    state, weight = lax.optimization_barrier((state, weight))
+    weight = lax.all_gather(weight, "head", axis=0, tiled=True)
     state = lax.all_to_all(
         state, "pool", split_axis=0, concat_axis=0, tiled=True, axis_index_groups=GROUPS
     )
@@ -288,14 +295,17 @@
         tiled=True,
         axis_index_groups=Y_GROUPS,
     )
-    partial = call(
+    vmem = pl.BlockSpec(memory_space=pltpu.VMEM)
+    partial = pl.pallas_call(
         project_kernel,
-        jax.ShapeDtypeStruct((NX, 2 * ROWS, out_weight.shape[1]), bf16),
-        blocks,
-        weight,
-        flops=2 * 64 * 8192 * 256,
-        moved=5 * 2**20,
-    )
+        out_shape=jax.ShapeDtypeStruct((NX, 2 * ROWS, out_weight.shape[1]), bf16),
+        in_specs=[pl.BlockSpec(memory_space=pltpu.SMEM), vmem, vmem],
+        out_specs=vmem,
+        compiler_params=pltpu.CompilerParams(vmem_limit_bytes=40 * 2**20),
+        cost_estimate=pl.CostEstimate(
+            flops=2 * 64 * 8192 * 256, bytes_accessed=5 * 2**20, transcendentals=0
+        ),
+    )((lax.axis_index("head") % NX * 2)[None], blocks, weight)
     partial = lax.all_to_all(
         partial, "pool", split_axis=0, concat_axis=0, tiled=True, axis_index_groups=X_GROUPS
     )

time: 122 us -> 122 us (level)
  the two profiles are of different devices: /device:TPU:384 before, /device:TPU:64 now
where the time goes in v4:
time: 122 us; the launch traced here: 121 us
  waiting for transfers between devices  52.6 us (43%)
  starting transfers between devices  27.8 us (23%)
  between operations  13.6 us (11%)
  Pallas kernels  10.7 us (9%)
  blocking collectives  8.36 us (7%)
  local copies, waits for them, and re-layouts  6.11 us (5%)
  other arithmetic  1.88 us (2%)
    all_to_all x1, waiting for transfers between devices, on_device(): lax.all_to_all(state, 'pool', split_axis=0, concat_axis=0, tiled=True, ax...  14.3 us
    ppermute x1, waiting for transfers between devices, on_device(): attention = lax.ppermute(attention, ('pool', 'head'), ATTENTION_MOVES)  14.3 us
    all_to_all x1, waiting for transfers between devices, on_device(): lax.all_to_all(jnp.broadcast_to(attention[None], (NY,) + attention.shape)...  12.4 us
    ppermute x1, waiting for transfers between devices, on_device(): weight = lax.ppermute(out_weight, ('pool', 'head'), WEIGHT_MOVES)  11.1 us
    pallas_call x5, Pallas kernels, call(): pl.pallas_call(kernel, out_shape=out_shape, compiler_params=pltpu.Compile...  9.82 us
    all_to_all x1, starting transfers between devices, on_device(): lax.all_to_all(jnp.broadcast_to(queries[None], (MEMBERS,) + queries.shape...  8.74 us
    all_to_all x1, blocking collectives, on_device(): lax.all_to_all(partial, 'pool', split_axis=0, concat_axis=0, tiled=True,...  8.36 us
    all_to_all x1, starting transfers between devices, on_device(): lax.all_to_all(state, 'pool', split_axis=0, concat_axis=0, tiled=True, ax...  6.36 us
  transfers between devices with their start and end apart: 7, of which 5 were waited for; matrix products, arithmetic and copies ran while one was open for 2% of the time, Pallas kernels for 2%

profile of v4, /device:TPU:64, one launch (start us, length us, event | category | flops | bytes accessed | tf_op | source)
XLA Modules:
  0.0 121.0 jit_solution(1716608159452102517)
XLA Ops:
  6.5 0.7 convert_bitcast_fusion
  7.2 1.1 fusion.1.own_ref
  8.3 0.0 copy-start.9
  8.3 0.0 copy-start.7
  8.3 3.5 %collective-permute-start.1 = (bf16[2064,128]{1,0:T(8,128)(2,1)S(1)}, bf16[2064,128]{1,0:T(8,128)(2,1)S(1)}, u32[]{:S(2)}, u32[]{:S(2)}) collective-permute-start(bf16[2064,128]{1,0:T(8,128)(2,1)S(1)} %fusion.1.own_ref), channel_id=1, source_target_pairs={{0,128},{16,144},{32,160},{48,176},{64,192},{80,208},{96,224},{112... | collective-permute-start | bytes 1585160 | tf_op jit(solution)/shard_map/ppermute | solution.py:217
  11.8 0.8 broadcast_in_dim.30
  12.7 8.7 %all-to-all-start = ((bf16[16,32,512]{2,1,0:T(8,128)(2,1)}), bf16[16,32,512]{2,1,0:T(8,128)(2,1)S(1)}, u32[]{:S(2)}, u32[]{:S(2)}) async-start(bf16[16,32,512]{2,1,0:T(8,128)(2,1)} %broadcast_in_dim.30), calls=%async_computation | async-start | bytes 1048576 | tf_op jit(solution)/shard_map/all_to_all | solution.py:219
  21.4 0.0 all-gather.2.cloned.1.call-start
  21.5 3.6 %collective-permute-start = (bf16[512,256]{1,0:T(8,128)(2,1)S(1)}, bf16[512,256]{1,0:T(8,128)(2,1)S(1)}, u32[]{:S(2)}, u32[]{:S(2)}) collective-permute-start(bf16[512,256]{1,0:T(8,128)(2,1)S(1)} %copy-done.9), channel_id=1, source_target_pairs={{0,0},{1,128},{2,256},{3,384},{4,4},{5,132},{6,260},{7,388},{8,8},... | collective-permute-start | bytes 786440 | tf_op jit(solution)/shard_map/ppermute | solution.py:227
  25.2 0.1 select_convert_fusion.hide_ref
  25.3 0.0 collective-permute-done.1.oth_ref
  25.3 0.2 shard_map.91
  25.6 1.0 copy-done.4
  26.6 11.1 %collective-permute-done = bf16[512,256]{1,0:T(8,128)(2,1)S(1)} collective-permute-done((bf16[512,256]{1,0:T(8,128)(2,1)S(1)}, bf16[512,256]{1,0:T(8,128)(2,1)S(1)}, u32[]{:S(2)}, u32[]{:S(2)}) %collective-permute-start) | collective-permute-done | bytes 262176 | tf_op jit(solution)/shard_map/ppermute | solution.py:227
  37.7 0.5 all-to-all-done.q_ref
  38.2 1.2 %copy-done.5 = bf16[2,1024,256]{2,1,0:T(8,128)(2,1)S(1)} copy-done((bf16[2,1024,256]{2,1,0:T(8,128)(2,1)S(1)}, bf16[2,1024,256]{2,1,0:T(8,128)(2,1)}, u32[]{:S(2)}) %copy-start.5) | copy-done | bytes 1048600
  39.4 7.2 %shard_map.92 = bf16[16,144,128]{2,1,0:T(8,128)(2,1)} custom-call(bf16[16,32,512]{2,1,0:T(8,128)(2,1)S(1)} %all-to-all-done.q_ref, bf16[512,128]{1,0:T(8,128)(2,1)S(1)} %select_convert_fusion.hide_ref, bf16[2,1024,256]{2,1,0:T(8,128)(2,1)S(1)} %copy-done.5, bf16[2,1024,128]{2,1,0:T(8,128)(2,1)S(1)} %get-tuple-element.31.values_ref), custom_call_target="tpu_custom_call" | custom-call | flops 2147483648 | bytes 2097152 | tf_op jit(solution)/shard_map/pallas_call | solution.py:187
  46.6 0.0 all-gather.2.cloned.1.call-update
  46.7 6.4 %all-to-all-start.1 = ((bf16[16,144,128]{2,1,0:T(8,128)(2,1)}), bf16[16,144,128]{2,1,0:T(8,128)(2,1)S(1)}, u32[]{:S(2)}, u32[]{:S(2)}) async-start(bf16[16,144,128]{2,1,0:T(8,128)(2,1)} %shard_map.92), calls=%async_computation.1 | async-start | bytes 1179648 | tf_op jit(solution)/shard_map/all_to_all | solution.py:276
  53.0 0.1 copy.10.len_ref
  53.1 1.1 shard_map.93
  54.3 14.3 %all-to-all-done.1.got_ref = bf16[16,144,128]{2,1,0:T(8,128)(2,1)S(1)} async-done(((bf16[16,144,128]{2,1,0:T(8,128)(2,1)}), bf16[16,144,128]{2,1,0:T(8,128)(2,1)S(1)}, u32[]{:S(2)}, u32[]{:S(2)}) %all-to-all-start.1) | async-done | bytes 589856 | tf_op jit(solution)/shard_map/all_to_all | solution.py:276
  68.6 0.6 shard_map.94
  69.2 2.1 %collective-permute-start.2 = (bf16[32,512]{1,0:T(8,128)(2,1)S(1)}, bf16[32,512]{1,0:T(8,128)(2,1)S(1)}, u32[]{:S(2)}, u32[]{:S(2)}) collective-permute-start(bf16[32,512]{1,0:T(8,128)(2,1)S(1)} %shard_map.94), channel_id=1, source_target_pairs={{0,0},{1,128},{2,256},{3,384},{4,112},{5,240},{6,368},{7,496},{8,9... | collective-permute-start | bytes 98312 | tf_op jit(solution)/shard_map/ppermute | solution.py:289
  71.3 14.3 %collective-permute-done.2 = bf16[32,512]{1,0:T(8,128)(2,1)S(1)} collective-permute-done((bf16[32,512]{1,0:T(8,128)(2,1)S(1)}, bf16[32,512]{1,0:T(8,128)(2,1)S(1)}, u32[]{:S(2)}, u32[]{:S(2)}) %collective-permute-start.2) | collective-permute-done | bytes 32800 | tf_op jit(solution)/shard_map/ppermute | solution.py:289
  85.6 0.7 broadcast_in_dim.34
  86.3 3.4 %all-to-all-start.2 = ((bf16[8,32,512]{2,1,0:T(8,128)(2,1)}), bf16[8,32,512]{2,1,0:T(8,128)(2,1)S(1)}, u32[]{:S(2)}, u32[]{:S(2)}) async-start(bf16[8,32,512]{2,1,0:T(8,128)(2,1)} %broadcast_in_dim.34), calls=%async_computation.2 | async-start | bytes 524288 | tf_op jit(solution)/shard_map/all_to_all | solution.py:290
  89.7 12.4 %all-to-all-done.2.att_ref = bf16[8,32,512]{2,1,0:T(8,128)(2,1)S(1)} async-done(((bf16[8,32,512]{2,1,0:T(8,128)(2,1)}), bf16[8,32,512]{2,1,0:T(8,128)(2,1)S(1)}, u32[]{:S(2)}, u32[]{:S(2)}) %all-to-all-start.2) | async-done | bytes 262176 | tf_op jit(solution)/shard_map/all_to_all | solution.py:290
  102.2 2.2 %copy-done = bf16[8192,256]{1,0:T(8,128)(2,1)S(1)} copy-done((bf16[8192,256]{1,0:T(8,128)(2,1)S(1)}, bf16[8192,256]{1,0:T(8,128)(2,1)}, u32[]{:S(2)}) %copy-start) | copy-done | bytes 4194328
  104.3 0.8 shard_map.95
  105.2 8.4 %all_to_all.20.part_ref = bf16[4,64,256]{2,1,0:T(8,128)(2,1)S(1)} all-to-all(bf16[4,64,256]{2,1,0:T(8,128)(2,1)S(1)} %shard_map.95), channel_id=1, replica_groups={{0,128,256,384},{16,144,272,400},{32,160,288,416},{48,176,304,432},{64,..., dimensions={0} | all-to-all | bytes 262144 | tf_op jit(solution)/shard_map/all_to_all | solution.py:309
  113.6 0.6 shard_map.96
  (18 shorter events, 0.0 us)
Async XLA Ops:
  6.5 5.3 %copy-start.3 = (bf16[32,512]{1,0:T(8,128)(2,1)S(1)}, bf16[32,512]{1,0:T(8,128)(2,1)}, u32[]{:S(2)}) copy-start(bf16[32,512]{1,0:T(8,128)(2,1)} %q_ref.1) | copy-start | bytes 98308
  8.3 13.2 %copy-start.9 = (bf16[512,256]{1,0:T(8,128)(2,1)S(1)}, bf16[512,256]{1,0:T(8,128)(2,1)}, u32[]{:S(2)}) copy-start(bf16[512,256]{1,0:T(8,128)(2,1)} %param.19) | copy-start | bytes 786436
  8.3 16.8 %copy-start.7 = (s32[1024]{0:T(1024)S(1)}, s32[1024]{0:T(1024)}, u32[]{:S(2)}) copy-start(s32[1024]{0:T(1024)} %param.12) | copy-start | bytes 12292
  8.3 17.0 %collective-permute-start.1 = (bf16[2064,128]{1,0:T(8,128)(2,1)S(1)}, bf16[2064,128]{1,0:T(8,128)(2,1)S(1)}, u32[]{:S(2)}, u32[]{:S(2)}) collective-permute-start(bf16[2064,128]{1,0:T(8,128)(2,1)S(1)} %fusion.1.own_ref), channel_id=1, source_target_pairs={{0,128},{16,144},{32,160},{48,176},{64,192},{80,208},{96,224},{112... | collective-permute-start | bytes 1585160 | tf_op jit(solution)/shard_map/ppermute | solution.py:217
  12.7 25.5 %all-to-all-start = ((bf16[16,32,512]{2,1,0:T(8,128)(2,1)}), bf16[16,32,512]{2,1,0:T(8,128)(2,1)S(1)}, u32[]{:S(2)}, u32[]{:S(2)}) async-start(bf16[16,32,512]{2,1,0:T(8,128)(2,1)} %broadcast_in_dim.30), calls=%async_computation | async-start | bytes 1048576 | tf_op jit(solution)/shard_map/all_to_all | solution.py:219
  21.4 80.7 %all-gather.2.cloned.1.call-start = ((), (), s32[]{:S(2)}) async-start(), calls=%async_computation.4 | async-start | bytes 4456448 | tf_op jit(solution)/shard_map/all_gather | solution.py:275
  21.5 16.2 %collective-permute-start = (bf16[512,256]{1,0:T(8,128)(2,1)S(1)}, bf16[512,256]{1,0:T(8,128)(2,1)S(1)}, u32[]{:S(2)}, u32[]{:S(2)}) collective-permute-start(bf16[512,256]{1,0:T(8,128)(2,1)S(1)} %copy-done.9), channel_id=1, source_target_pairs={{0,0},{1,128},{2,256},{3,384},{4,4},{5,132},{6,260},{7,388},{8,8},... | collective-permute-start | bytes 786440 | tf_op jit(solution)/shard_map/ppermute | solution.py:227
  25.6 1.0 copy-start.4
  37.7 8.9 %copy-start.6 = (bf16[512,256]{1,0:T(8,128)(2,1)}, bf16[512,256]{1,0:T(8,128)(2,1)S(1)}, u32[]{:S(2)}) copy-start(bf16[512,256]{1,0:T(8,128)(2,1)S(1)} %collective-permute-done) | copy-start | bytes 786436
  38.2 1.2 %copy-start.5 = (bf16[2,1024,256]{2,1,0:T(8,128)(2,1)S(1)}, bf16[2,1024,256]{2,1,0:T(8,128)(2,1)}, u32[]{:S(2)}) copy-start(bf16[2,1024,256]{2,1,0:T(8,128)(2,1)} %copy-done.4) | copy-start | bytes 3145732
  39.4 13.7 %copy-start.2 = (bf16[1,32,128,128]{3,2,1,0:T(8,128)(2,1)S(1)}, bf16[1,32,128,128]{3,2,1,0:T(8,128)(2,1)}, u32[]{:S(2)}) copy-start(bf16[1,32,128,128]{3,2,1,0:T(8,128)(2,1)} %param.18) | copy-start | bytes 3145732
  46.6 6.4 %copy-start.8 = (s32[32]{0:T(128)S(1)}, s32[32]{0:T(128)}, u32[]{:S(2)}) copy-start(s32[32]{0:T(128)} %param.14) | copy-start | bytes 388
  46.6 6.5 %copy-start.1 = (bf16[1,32,128,128]{3,2,1,0:T(8,128)(2,1)S(1)}, bf16[1,32,128,128]{3,2,1,0:T(8,128)(2,1)}, u32[]{:S(2)}) copy-start(bf16[1,32,128,128]{3,2,1,0:T(8,128)(2,1)} %param.17) | copy-start | bytes 3145732
  46.7 21.9 %all-to-all-start.1 = ((bf16[16,144,128]{2,1,0:T(8,128)(2,1)}), bf16[16,144,128]{2,1,0:T(8,128)(2,1)S(1)}, u32[]{:S(2)}, u32[]{:S(2)}) async-start(bf16[16,144,128]{2,1,0:T(8,128)(2,1)} %shard_map.92), calls=%async_computation.1 | async-start | bytes 1179648 | tf_op jit(solution)/shard_map/all_to_all | solution.py:276
  69.2 16.4 %collective-permute-start.2 = (bf16[32,512]{1,0:T(8,128)(2,1)S(1)}, bf16[32,512]{1,0:T(8,128)(2,1)S(1)}, u32[]{:S(2)}, u32[]{:S(2)}) collective-permute-start(bf16[32,512]{1,0:T(8,128)(2,1)S(1)} %shard_map.94), channel_id=1, source_target_pairs={{0,0},{1,128},{2,256},{3,384},{4,112},{5,240},{6,368},{7,496},{8,9... | collective-permute-start | bytes 98312 | tf_op jit(solution)/shard_map/ppermute | solution.py:289
  86.3 15.8 %all-to-all-start.2 = ((bf16[8,32,512]{2,1,0:T(8,128)(2,1)}), bf16[8,32,512]{2,1,0:T(8,128)(2,1)S(1)}, u32[]{:S(2)}, u32[]{:S(2)}) async-start(bf16[8,32,512]{2,1,0:T(8,128)(2,1)} %broadcast_in_dim.34), calls=%async_computation.2 | async-start | bytes 524288 | tf_op jit(solution)/shard_map/all_to_all | solution.py:290
  102.2 2.2 %copy-start = (bf16[8192,256]{1,0:T(8,128)(2,1)S(1)}, bf16[8192,256]{1,0:T(8,128)(2,1)}, u32[]{:S(2)}) copy-start(bf16[8192,256]{1,0:T(8,128)(2,1)} %all-gather.2.cloned.1.call-done.w_ref) | copy-start | bytes 12582916
Sparse Core Ops, SparseCore 0:
  46.8 46.3 all-gather.1

commit v5 on v4

--- a/solution.py
+++ b/solution.py
@@ -237,6 +237,7 @@
         moved=2 * 2**20,
     )
     got, weight, keys, values = lax.optimization_barrier((got, weight, keys, values))
+    weight = lax.all_gather(weight, "head", axis=0, tiled=True)
 
     span = NY * ROWS
     outer = (x == GROUP_X[0][0]) | (x == GROUP_X[0][1])
@@ -271,8 +272,6 @@
         flops=4 * 2048 * 2048 * 128,
         moved=2 * 2**20,
     )
-    state, weight = lax.optimization_barrier((state, weight))
-    weight = lax.all_gather(weight, "head", axis=0, tiled=True)
     state = lax.all_to_all(
         state, "pool", split_axis=0, concat_axis=0, tiled=True, axis_index_groups=GROUPS
     )

time: 122 us -> 122 us (level)
    unnamed x20 -> x18, local copies, waits for them, and re-layouts: 4.43 us -> 4.65 us
  transfers between devices with their start and end apart: 7 -> 7, of which waited for: 5 -> 5; matrix products, arithmetic and copies ran while one was open for 2% -> 1% of each run, Pallas kernels for 2% -> 8%
where the time goes in v5:
time: 122 us
  waiting for transfers between devices  52.9 us (43%)
  starting transfers between devices  27.9 us (23%)
  between operations  13.6 us (11%)
  Pallas kernels  10.6 us (9%)
  blocking collectives  8.36 us (7%)
  local copies, waits for them, and re-layouts  6.33 us (5%)
  other arithmetic  1.88 us (2%)
    all_to_all x1, waiting for transfers between devices, on_device(): lax.all_to_all(state, 'pool', split_axis=0, concat_axis=0, tiled=True, ax...  14.4 us
    ppermute x1, waiting for transfers between devices, on_device(): attention = lax.ppermute(attention, ('pool', 'head'), ATTENTION_MOVES)  14.1 us
    all_to_all x1, waiting for transfers between devices, on_device(): lax.all_to_all(jnp.broadcast_to(attention[None], (NY,) + attention.shape)...  12.4 us
    ppermute x1, waiting for transfers between devices, on_device(): weight = lax.ppermute(out_weight, ('pool', 'head'), WEIGHT_MOVES)  11.5 us
    pallas_call x5, Pallas kernels, call(): pl.pallas_call(kernel, out_shape=out_shape, compiler_params=pltpu.Compile...  9.8 us
    all_to_all x1, starting transfers between devices, on_device(): lax.all_to_all(jnp.broadcast_to(queries[None], (MEMBERS,) + queries.shape...  8.74 us
    all_to_all x1, blocking collectives, on_device(): lax.all_to_all(partial, 'pool', split_axis=0, concat_axis=0, tiled=True,...  8.36 us
    all_to_all x1, starting transfers between devices, on_device(): lax.all_to_all(state, 'pool', split_axis=0, concat_axis=0, tiled=True, ax...  6.7 us
  transfers between devices with their start and end apart: 7, of which 5 were waited for; matrix products, arithmetic and copies ran while one was open for 1% of the time, Pallas kernels for 8%

profile of v5, /device:TPU:64, one launch (start us, length us, event | category | flops | bytes accessed | tf_op | source)
XLA Modules:
  0.0 121.6 jit_solution(5783179193185535364)
XLA Ops:
  6.5 0.7 convert_bitcast_fusion
  7.2 1.1 fusion.1.own_ref
  8.3 3.4 %collective-permute-start.1 = (bf16[2064,128]{1,0:T(8,128)(2,1)S(1)}, bf16[2064,128]{1,0:T(8,128)(2,1)S(1)}, u32[]{:S(2)}, u32[]{:S(2)}) collective-permute-start(bf16[2064,128]{1,0:T(8,128)(2,1)S(1)} %fusion.1.own_ref), channel_id=1, source_target_pairs={{0,128},{16,144},{32,160},{48,176},{64,192},{80,208},{96,224},{112... | collective-permute-start | bytes 1585160 | tf_op jit(solution)/shard_map/ppermute | solution.py:217
  11.7 0.9 broadcast_in_dim.30
  12.5 8.7 %all-to-all-start = ((bf16[16,32,512]{2,1,0:T(8,128)(2,1)}), bf16[16,32,512]{2,1,0:T(8,128)(2,1)S(1)}, u32[]{:S(2)}, u32[]{:S(2)}) async-start(bf16[16,32,512]{2,1,0:T(8,128)(2,1)} %broadcast_in_dim.30), calls=%async_computation | async-start | bytes 1048576 | tf_op jit(solution)/shard_map/all_to_all | solution.py:219
  21.3 0.0 copy-start.7
  21.3 0.0 all-gather.2.cloned.1.call-start
  21.4 3.6 %collective-permute-start = (bf16[512,256]{1,0:T(8,128)(2,1)}, bf16[512,256]{1,0:T(8,128)(2,1)S(1)}, u32[]{:S(2)}, u32[]{:S(2)}) collective-permute-start(bf16[512,256]{1,0:T(8,128)(2,1)} %param.19), channel_id=1, source_target_pairs={{0,0},{1,128},{2,256},{3,384},{4,4},{5,132},{6,260},{7,388},{8,8},... | collective-permute-start | bytes 786440 | tf_op jit(solution)/shard_map/ppermute | solution.py:227
  25.0 0.0 collective-permute-done.1.oth_ref
  25.0 0.2 shard_map.91
  25.3 1.0 copy-done.4
  26.2 11.5 %collective-permute-done = bf16[512,256]{1,0:T(8,128)(2,1)S(1)} collective-permute-done((bf16[512,256]{1,0:T(8,128)(2,1)}, bf16[512,256]{1,0:T(8,128)(2,1)S(1)}, u32[]{:S(2)}, u32[]{:S(2)}) %collective-permute-start) | collective-permute-done | bytes 262176 | tf_op jit(solution)/shard_map/ppermute | solution.py:227
  37.7 0.4 all-to-all-done.q_ref
  38.2 0.2 copy-done.6
  38.4 0.0 all-gather.2.cloned.1.call-update
  38.5 0.1 select_convert_fusion.hide_ref
  38.7 1.2 copy-done.5
  39.9 7.2 %shard_map.92 = bf16[16,144,128]{2,1,0:T(8,128)(2,1)} custom-call(bf16[16,32,512]{2,1,0:T(8,128)(2,1)S(1)} %all-to-all-done.q_ref, bf16[512,128]{1,0:T(8,128)(2,1)S(1)} %select_convert_fusion.hide_ref, bf16[2,1024,256]{2,1,0:T(8,128)(2,1)S(1)} %copy-done.5, bf16[2,1024,128]{2,1,0:T(8,128)(2,1)S(1)} %get-tuple-element.29.values_ref), custom_call_target="tpu_custom_call" | custom-call | flops 2147483648 | bytes 2097152 | tf_op jit(solution)/shard_map/pallas_call | solution.py:187
  47.1 6.7 %all-to-all-start.1 = ((bf16[16,144,128]{2,1,0:T(8,128)(2,1)}), bf16[16,144,128]{2,1,0:T(8,128)(2,1)S(1)}, u32[]{:S(2)}, u32[]{:S(2)}) async-start(bf16[16,144,128]{2,1,0:T(8,128)(2,1)} %shard_map.92), calls=%async_computation.1 | async-start | bytes 1179648 | tf_op jit(solution)/shard_map/all_to_all | solution.py:275
  53.8 0.1 copy.10.len_ref
  53.9 1.1 shard_map.93
  55.0 14.4 %all-to-all-done.1.got_ref = bf16[16,144,128]{2,1,0:T(8,128)(2,1)S(1)} async-done(((bf16[16,144,128]{2,1,0:T(8,128)(2,1)}), bf16[16,144,128]{2,1,0:T(8,128)(2,1)S(1)}, u32[]{:S(2)}, u32[]{:S(2)}) %all-to-all-start.1) | async-done | bytes 589856 | tf_op jit(solution)/shard_map/all_to_all | solution.py:275
  69.4 0.6 shard_map.94
  70.0 2.0 %collective-permute-start.2 = (bf16[32,512]{1,0:T(8,128)(2,1)S(1)}, bf16[32,512]{1,0:T(8,128)(2,1)S(1)}, u32[]{:S(2)}, u32[]{:S(2)}) collective-permute-start(bf16[32,512]{1,0:T(8,128)(2,1)S(1)} %shard_map.94), channel_id=1, source_target_pairs={{0,0},{1,128},{2,256},{3,384},{4,112},{5,240},{6,368},{7,496},{8,9... | collective-permute-start | bytes 98312 | tf_op jit(solution)/shard_map/ppermute | solution.py:288
  72.0 14.1 %collective-permute-done.2 = bf16[32,512]{1,0:T(8,128)(2,1)S(1)} collective-permute-done((bf16[32,512]{1,0:T(8,128)(2,1)S(1)}, bf16[32,512]{1,0:T(8,128)(2,1)S(1)}, u32[]{:S(2)}, u32[]{:S(2)}) %collective-permute-start.2) | collective-permute-done | bytes 32800 | tf_op jit(solution)/shard_map/ppermute | solution.py:288
  86.2 0.7 broadcast_in_dim.34
  86.9 3.4 %all-to-all-start.2 = ((bf16[8,32,512]{2,1,0:T(8,128)(2,1)}), bf16[8,32,512]{2,1,0:T(8,128)(2,1)S(1)}, u32[]{:S(2)}, u32[]{:S(2)}) async-start(bf16[8,32,512]{2,1,0:T(8,128)(2,1)} %broadcast_in_dim.34), calls=%async_computation.2 | async-start | bytes 524288 | tf_op jit(solution)/shard_map/all_to_all | solution.py:289
  90.3 12.4 %all-to-all-done.2.att_ref = bf16[8,32,512]{2,1,0:T(8,128)(2,1)S(1)} async-done(((bf16[8,32,512]{2,1,0:T(8,128)(2,1)}), bf16[8,32,512]{2,1,0:T(8,128)(2,1)S(1)}, u32[]{:S(2)}, u32[]{:S(2)}) %all-to-all-start.2) | async-done | bytes 262176 | tf_op jit(solution)/shard_map/all_to_all | solution.py:289
  102.7 2.2 %copy-done = bf16[8192,256]{1,0:T(8,128)(2,1)S(1)} copy-done((bf16[8192,256]{1,0:T(8,128)(2,1)S(1)}, bf16[8192,256]{1,0:T(8,128)(2,1)}, u32[]{:S(2)}) %copy-start) | copy-done | bytes 4194328
  104.9 0.8 shard_map.95
  105.8 8.4 %all_to_all.20.part_ref = bf16[4,64,256]{2,1,0:T(8,128)(2,1)S(1)} all-to-all(bf16[4,64,256]{2,1,0:T(8,128)(2,1)S(1)} %shard_map.95), channel_id=1, replica_groups={{0,128,256,384},{16,144,272,400},{32,160,288,416},{48,176,304,432},{64,..., dimensions={0} | all-to-all | bytes 262144 | tf_op jit(solution)/shard_map/all_to_all | solution.py:308
  114.1 0.6 shard_map.96
  (16 shorter events, 0.0 us)
Async XLA Ops:
  6.5 5.2 %copy-start.3 = (bf16[32,512]{1,0:T(8,128)(2,1)S(1)}, bf16[32,512]{1,0:T(8,128)(2,1)}, u32[]{:S(2)}) copy-start(bf16[32,512]{1,0:T(8,128)(2,1)} %q_ref.1) | copy-start | bytes 98308
  8.3 16.7 %collective-permute-start.1 = (bf16[2064,128]{1,0:T(8,128)(2,1)S(1)}, bf16[2064,128]{1,0:T(8,128)(2,1)S(1)}, u32[]{:S(2)}, u32[]{:S(2)}) collective-permute-start(bf16[2064,128]{1,0:T(8,128)(2,1)S(1)} %fusion.1.own_ref), channel_id=1, source_target_pairs={{0,128},{16,144},{32,160},{48,176},{64,192},{80,208},{96,224},{112... | collective-permute-start | bytes 1585160 | tf_op jit(solution)/shard_map/ppermute | solution.py:217
  12.5 25.6 %all-to-all-start = ((bf16[16,32,512]{2,1,0:T(8,128)(2,1)}), bf16[16,32,512]{2,1,0:T(8,128)(2,1)S(1)}, u32[]{:S(2)}, u32[]{:S(2)}) async-start(bf16[16,32,512]{2,1,0:T(8,128)(2,1)} %broadcast_in_dim.30), calls=%async_computation | async-start | bytes 1048576 | tf_op jit(solution)/shard_map/all_to_all | solution.py:219
  21.3 17.2 %copy-start.7 = (s32[1024]{0:T(1024)S(1)}, s32[1024]{0:T(1024)}, u32[]{:S(2)}) copy-start(s32[1024]{0:T(1024)} %param.12) | copy-start | bytes 12292
  21.3 81.4 %all-gather.2.cloned.1.call-start = ((), (), s32[]{:S(2)}) async-start(), calls=%async_computation.4 | async-start | bytes 4456448 | tf_op jit(solution)/shard_map/all_gather | solution.py:240
  21.4 16.4 %collective-permute-start = (bf16[512,256]{1,0:T(8,128)(2,1)}, bf16[512,256]{1,0:T(8,128)(2,1)S(1)}, u32[]{:S(2)}, u32[]{:S(2)}) collective-permute-start(bf16[512,256]{1,0:T(8,128)(2,1)} %param.19), channel_id=1, source_target_pairs={{0,0},{1,128},{2,256},{3,384},{4,4},{5,132},{6,260},{7,388},{8,8},... | collective-permute-start | bytes 786440 | tf_op jit(solution)/shard_map/ppermute | solution.py:227
  25.3 1.0 copy-start.4
  37.7 0.7 copy-start.6
  38.6 1.2 %copy-start.5 = (bf16[2,1024,256]{2,1,0:T(8,128)(2,1)S(1)}, bf16[2,1024,256]{2,1,0:T(8,128)(2,1)}, u32[]{:S(2)}) copy-start(bf16[2,1024,256]{2,1,0:T(8,128)(2,1)} %copy-done.4) | copy-start | bytes 3145732
  39.9 14.0 %copy-start.2 = (bf16[1,32,128,128]{3,2,1,0:T(8,128)(2,1)S(1)}, bf16[1,32,128,128]{3,2,1,0:T(8,128)(2,1)}, u32[]{:S(2)}) copy-start(bf16[1,32,128,128]{3,2,1,0:T(8,128)(2,1)} %param.18) | copy-start | bytes 3145732
  47.1 6.7 %copy-start.8 = (s32[32]{0:T(128)S(1)}, s32[32]{0:T(128)}, u32[]{:S(2)}) copy-start(s32[32]{0:T(128)} %param.14) | copy-start | bytes 388
  47.1 6.8 %copy-start.1 = (bf16[1,32,128,128]{3,2,1,0:T(8,128)(2,1)S(1)}, bf16[1,32,128,128]{3,2,1,0:T(8,128)(2,1)}, u32[]{:S(2)}) copy-start(bf16[1,32,128,128]{3,2,1,0:T(8,128)(2,1)} %param.17) | copy-start | bytes 3145732
  47.1 22.3 %all-to-all-start.1 = ((bf16[16,144,128]{2,1,0:T(8,128)(2,1)}), bf16[16,144,128]{2,1,0:T(8,128)(2,1)S(1)}, u32[]{:S(2)}, u32[]{:S(2)}) async-start(bf16[16,144,128]{2,1,0:T(8,128)(2,1)} %shard_map.92), calls=%async_computation.1 | async-start | bytes 1179648 | tf_op jit(solution)/shard_map/all_to_all | solution.py:275
  70.0 16.1 %collective-permute-start.2 = (bf16[32,512]{1,0:T(8,128)(2,1)S(1)}, bf16[32,512]{1,0:T(8,128)(2,1)S(1)}, u32[]{:S(2)}, u32[]{:S(2)}) collective-permute-start(bf16[32,512]{1,0:T(8,128)(2,1)S(1)} %shard_map.94), channel_id=1, source_target_pairs={{0,0},{1,128},{2,256},{3,384},{4,112},{5,240},{6,368},{7,496},{8,9... | collective-permute-start | bytes 98312 | tf_op jit(solution)/shard_map/ppermute | solution.py:288
  86.9 15.8 %all-to-all-start.2 = ((bf16[8,32,512]{2,1,0:T(8,128)(2,1)}), bf16[8,32,512]{2,1,0:T(8,128)(2,1)S(1)}, u32[]{:S(2)}, u32[]{:S(2)}) async-start(bf16[8,32,512]{2,1,0:T(8,128)(2,1)} %broadcast_in_dim.34), calls=%async_computation.2 | async-start | bytes 524288 | tf_op jit(solution)/shard_map/all_to_all | solution.py:289
  102.7 2.2 %copy-start = (bf16[8192,256]{1,0:T(8,128)(2,1)S(1)}, bf16[8192,256]{1,0:T(8,128)(2,1)}, u32[]{:S(2)}) copy-start(bf16[8192,256]{1,0:T(8,128)(2,1)} %all-gather.2.cloned.1.call-done.w_ref) | copy-start | bytes 12582916
Sparse Core Ops, SparseCore 0:
  38.6 47.0 all-gather.1
